TPU v7x, 256 devices: a whole 4x4x8 slice. The times are simulated.
256 devices in a mesh: item: 8 (over y, x_hi), user: 32 (over x_lo, z, core).
Axes of the slice: x: 4 (x_hi: 2, x_lo: 2; x = x_hi * 2 + x_lo), y: 4, z: 8, core: 2. Of those that a mesh axis runs over, the one named last changes fastest.
Arguments:
- user_vecs: bfloat16 [8192, 128], P('user'), may hold values from -15 to 15
- row_weight: bfloat16 [8192], P('user'), may hold values from 0.25 to 4
- positive: int32 [8192], P('user'), may hold values from 0 to 131071
- item_feats: bfloat16 [131072, 128], P(('item', 'user')), may hold values from -6 to 6
- valid: int32 [131072], P(('item', 'user')), may hold values from 0 to 1, as said below
- w_in: bfloat16 [128, 1024], replicated, may hold values from -0.5 to 0.5
- w_out: bfloat16 [1024, 128], replicated, may hold values from -0.1875 to 0.1875
Outputs:
- grad_user: float32 [8192, 128], P('user')
- grad_item: float32 [131072, 128], P(('item', 'user'))
- grad_w_in: float32 [128, 1024], replicated
- grad_w_out: float32 [1024, 128], replicated
Inputs may be any that keep to these rules, and one draw needn't show every extreme that they name: `valid`: each aligned block of 16384 items has its own rate of ones, between a quarter and all.
All inputs are finite; a program needn't handle non-finite values.
Results may differ from a plain program's by a relative error of at most 0.012.
The roundings to bfloat16 on the way count: a program that leaves them out, or rounds other values in their place, can miss the bound.
Values may be sent and summed in bfloat16 or wider, within the bound.
A program may use at most 128 MiB of HBM per device.

v0:
```python
import jax
import jax.numpy as jnp
from jax import lax
from jax.sharding import PartitionSpec as P

neg_floor = -1e30


def tower(item_feats, w_in, w_out):
    pre_act = jnp.dot(item_feats, w_in, preferred_element_type=jnp.float32)
    hidden = jax.nn.silu(pre_act).astype(jnp.bfloat16)
    item_vec = (
        item_feats.astype(jnp.float32) + jnp.dot(hidden, w_out, preferred_element_type=jnp.float32)
    ).astype(jnp.bfloat16)
    return (pre_act, hidden, item_vec)


def block_terms(users, positive, vec_block, valid_block, first_item):
    scores = jnp.dot(users, vec_block.T, preferred_element_type=jnp.float32)
    item_ids = first_item + jnp.arange(vec_block.shape[0], dtype=jnp.int32)
    is_positive = item_ids[None, :] == positive[:, None]
    live_mask = (valid_block == 1)[None, :] | is_positive
    return (scores, is_positive, live_mask)


def block_stats(scores, live_mask):
    row_peak = jnp.max(jnp.where(live_mask, scores, neg_floor), axis=1)
    expo = jnp.where(live_mask, jnp.exp(scores - row_peak[:, None]), 0.0)
    return (row_peak, jnp.sum(expo, axis=1))


def merge_stats(first, second):
    peak_new = jnp.maximum(first[0], second[0])
    return (
        peak_new,
        first[1] * jnp.exp(first[0] - peak_new) + second[1] * jnp.exp(second[0] - peak_new),
    )


def block_grad(scores, is_positive, live_mask, row_peak, row_total, weights):
    expo = jnp.where(live_mask, jnp.exp(scores - row_peak[:, None]), 0.0)
    return (
        weights.astype(jnp.float32)[:, None]
        * (expo / row_total[:, None] - is_positive.astype(jnp.float32))
    ).astype(jnp.bfloat16)


def body(user_vecs, row_weight, positive, item_feats, valid, w_in, w_out):
    pre_act, hidden, item_vec = tower(item_feats, w_in, w_out)
    width = item_feats.shape[1]
    shard_vec, shard_valid = (
        lax.all_gather(item_vec, "user", axis=0, tiled=True),
        lax.all_gather(valid, "user", axis=0, tiled=True),
    )
    shard_rows = shard_vec.shape[0]
    start_item = lax.axis_index("item") * shard_rows
    block_size = min(2048, shard_rows)
    block_count = shard_rows // block_size
    vec_blocks = shard_vec.reshape(block_count, block_size, width)
    valid_blocks = shard_valid.reshape(block_count, block_size)
    first_items = start_item + block_size * jnp.arange(block_count, dtype=jnp.int32)
    user_count = user_vecs.shape[0]

    def stats_step(running, blk):
        vec_block, valid_block, first_item = blk
        scores, is_positive, live_mask = block_terms(
            user_vecs, positive, vec_block, valid_block, first_item
        )
        return (merge_stats(running, block_stats(scores, live_mask)), None)

    start_stats = (
        jnp.full((user_count,), neg_floor, jnp.float32),
        jnp.zeros((user_count,), jnp.float32),
    )
    (part_peak, part_total), unused = lax.scan(
        stats_step, start_stats, (vec_blocks, valid_blocks, first_items)
    )
    row_peak = lax.pmax(part_peak, "item")
    row_total = lax.psum(part_total * jnp.exp(part_peak - row_peak), "item")

    def grad_step(accum, blk):
        vec_block, valid_block, first_item = blk
        scores, is_positive, live_mask = block_terms(
            user_vecs, positive, vec_block, valid_block, first_item
        )
        grad_scores = block_grad(scores, is_positive, live_mask, row_peak, row_total, row_weight)
        accum = accum + jnp.dot(grad_scores, vec_block, preferred_element_type=jnp.float32)
        return (accum, jnp.dot(grad_scores.T, user_vecs, preferred_element_type=jnp.float32))

    user_part, item_terms = lax.scan(
        grad_step,
        jnp.zeros((user_count, width), jnp.float32),
        (vec_blocks, valid_blocks, first_items),
    )
    item_grad = lax.psum_scatter(
        item_terms.reshape(shard_rows, width), "user", scatter_dimension=0, tiled=True
    )
    grad_user = lax.psum(user_part, "item")
    grad_vec = item_grad.astype(jnp.bfloat16)
    grad_w_out = jnp.dot(hidden.T, grad_vec, preferred_element_type=jnp.float32)
    back_hidden = jnp.dot(grad_vec, w_out.T, preferred_element_type=jnp.float32)
    sigma = jax.nn.sigmoid(pre_act)
    grad_pre = (back_hidden * (sigma * (1.0 + pre_act * (1.0 - sigma)))).astype(jnp.bfloat16)
    grad_w_in = jnp.dot(item_feats.T, grad_pre, preferred_element_type=jnp.float32)
    grad_item = grad_vec.astype(jnp.float32) + jnp.dot(
        grad_pre, w_in.T, preferred_element_type=jnp.float32
    )
    grad_w_in, grad_w_out = lax.psum((grad_w_in, grad_w_out), ("item", "user"))
    return (grad_user, grad_item, grad_w_in, grad_w_out)


def solution(mesh):
    return jax.shard_map(
        body,
        mesh=mesh,
        in_specs=(
            P("user", None),
            P("user"),
            P("user"),
            P(("item", "user"), None),
            P(("item", "user")),
            P(),
            P(),
        ),
        out_specs=(P("user", None), P(("item", "user"), None), P(), P()),
        check_vma=False,
    )
```

profile of v0, /device:TPU:1, one launch (start us, length us, event | category | flops | bytes accessed | tf_op | source)
XLA Modules:
  0.0 695.5 jit_solution(18313222764081051569)
XLA Ops:
  8.1 2.9 multiply_convert_fusion.1
  12.2 39.0 %all-gather = s32[32,1,512]{2,1,0:T(1,128)S(1)} all-gather(s32[1,1,512]{2,1,0:T(1,128)S(1)} %bitcast.75), channel_id=1, replica_groups=mesh['item'=8,'user'=32] {'user'}, dimensions={0}, use_global_device_ids=true | all-gather | bytes 67584 | tf_op jit(solution)/shard_map/all_gather | solution.py:53
  51.5 31.8 %all-gather.3.cloned.1.call-done = bf16[16384,128]{1,0:T(8,128)(2,1)} async-done(((bf16[512,128]{1,0:T(8,128)(2,1)}), bf16[16384,128]{1,0:T(8,128)(2,1)}) %all-gather.3.cloned.1.call-update) | async-done | bytes 4194320 | tf_op jit(solution)/shard_map/all_gather | solution.py:52
  83.3 36.4 %while.26 = (s32[]{:T(128)}, f32[256]{0:T(256)S(1)}, f32[256]{0:T(256)S(1)}, s32[8,2048]{1,0:T(8,128)S(1)}, s32[8]{0:T(128)S(1)}, /*index=5*/s32[256]{0:T(256)S(...) while((s32[]{:T(128)}, f32[256]{0:T(256)S(1)}, ...), condition=%wide.region_3.4_spmd.clone, body=%wide.region_0.3_spmd.clone.sunk | while | flops 138941952 | bytes 4834947 | solution.py:75
  84.6 1.8 select_reduce_fusion.4
  89.2 1.8 select_reduce_fusion.4
  93.7 1.8 select_reduce_fusion.4
  98.3 1.8 select_reduce_fusion.4
  102.8 1.8 select_reduce_fusion.4
  107.4 1.8 select_reduce_fusion.4
  111.9 1.8 select_reduce_fusion.4
  116.5 1.8 select_reduce_fusion.4
  119.7 20.3 %pmax.7 = f32[256]{0:T(256)S(1)} all-reduce(f32[256]{0:T(256)S(1)} %get-tuple-element.105), channel_id=1, replica_groups=mesh['item'=8,'user'=32] {'item'}, use_global_device_ids=true, to_apply=%region_4.5 | all-reduce | flops 256 | bytes 2048 | tf_op jit(solution)/shard_map/pmax | solution.py:78
  140.1 15.6 %psum.28 = f32[256]{0:T(256)S(1)} all-reduce(f32[256]{0:T(256)S(1)} %exponential_multiply_fusion), channel_id=1, replica_groups=mesh['item'=8,'user'=32] {'item'}, use_global_device_ids=true, to_apply=%region_5.6 | all-reduce | flops 256 | bytes 2048 | tf_op jit(solution)/shard_map/psum | solution.py:79
  155.6 51.7 %while.27 = (s32[]{:T(128)}, f32[256,128]{1,0:T(8,128)S(1)}, f32[8,2048,128]{2,1,0:T(8,128)}, bf16[256]{0:T(256)(128)(2,1)S(1)}, s32[8,2048]{1,0:T(8,128)S(1)}, ...) while((s32[]{:T(128)}, f32[256,128]{1,0:T(8,128)S(1)}, ...), condition=%wide.region_7.8_spmd.clone, body=%wide.region_6.7_spmd.clone.sunk | while | flops 407441664 | bytes 5672091 | solution.py:90
  156.9 2.1 fusion.57
  163.4 2.2 fusion.57
  167.0 1.6 convolution_add_fusion.4
  169.9 2.2 fusion.57
  176.4 2.1 fusion.57
  182.8 2.2 fusion.57
  186.4 1.6 convolution_add_fusion.4
  189.2 2.2 fusion.57
  195.8 2.2 fusion.57
  202.2 2.2 fusion.57
  208.0 129.3 %reduce-scatter.2.cloned.1.call-done = f32[512,128]{1,0:T(8,128)} async-done(((f32[16384,128]{1,0:T(8,128)}), f32[512,128]{1,0:T(8,128)}) %reduce-scatter.2.cloned.1.call-update) | async-done | bytes 262160 | tf_op jit(solution)/shard_map/reduce_scatter | solution.py:95
  337.3 2.6 multiply_convert_fusion
  344.2 254.3 %all-reduce.6.cloned.1.call-done = (f32[128,1024]{0,1:T(8,128)}, f32[1024,128]{1,0:T(8,128)}) async-done(((f32[128,1024]{0,1:T(8,128)}, f32[1024,128]{1,0:T(8,128)}), (f32[128,1024]{0,1:T(8,128)}, f32[1024,128]{1,0:T(8,128)})) %all-reduce.6.cloned.1.call-update) | async-done | bytes 1048592 | tf_op jit(solution)/shard_map/psum | solution.py:108
  598.5 2.0 copy.12
  600.6 85.0 %all-reduce.4.cloned.1.call-done = f32[256,128]{1,0:T(8,128)} async-done(((f32[256,128]{1,0:T(8,128)}), f32[256,128]{1,0:T(8,128)}) %all-reduce.4.cloned.1.call-update) | async-done | bytes 131088 | tf_op jit(solution)/shard_map/psum | solution.py:98
  685.5 1.6 copy.35
  687.1 1.9 copy.36
  (124 shorter events, 60.2 us)
Async XLA Ops:
  7.2 1.0 copy-start
  7.2 3.8 copy-start.4
  7.2 3.8 copy-start.5
  7.2 5.0 copy-start.7
  7.2 76.1 %copy-start.2 = (bf16[256,128]{1,0:T(8,128)(2,1)S(1)}, bf16[256,128]{1,0:T(8,128)(2,1)}, u32[]{:S(2)}) copy-start(bf16[256,128]{1,0:T(8,128)(2,1)} %param.11) | copy-start | bytes 196612
  7.2 76.1 %copy-start.6 = (s32[256]{0:T(256)S(1)}, s32[256]{0:T(256)}, u32[]{:S(2)}) copy-start(s32[256]{0:T(256)} %param.13) | copy-start | bytes 3076
  7.2 76.1 %all-gather.3.cloned.1.call-start = ((), (), s32[]{:S(2)}) async-start(), calls=%async_computation.1 | async-start | bytes 4325376 | tf_op jit(solution)/shard_map/all_gather | solution.py:52
  12.1 325.2 %reduce-scatter.2.cloned.1.call-start = ((), (), s32[]{:S(2)}) async-start(), calls=%async_computation.3 | async-start | bytes 8650752 | tf_op jit(solution)/shard_map/reduce_scatter | solution.py:95
  83.3 72.3 %copy-start.8 = (bf16[256]{0:T(256)(128)(2,1)S(1)}, bf16[256]{0:T(256)(128)(2,1)}, u32[]{:S(2)}) copy-start(bf16[256]{0:T(256)(128)(2,1)} %param.12) | copy-start | bytes 1540
  207.4 0.7 copy-start.1
  208.0 390.5 %all-reduce.6.cloned.1.call-start = ((), (), s32[]{:S(2)}) async-start(), calls=%async_computation.4 | async-start | bytes 2097152 | tf_op jit(solution)/shard_map/psum | solution.py:108
  337.3 3.8 copy-start.3
  342.5 343.1 %all-reduce.4.cloned.1.call-start = ((), (), s32[]{:S(2)}) async-start(), calls=%async_computation.2 | async-start | bytes 262144 | tf_op jit(solution)/shard_map/psum | solution.py:98
Sparse Core Ops, SparseCore 0:
  12.3 71.0 all-gather.2
  207.5 129.7 reduce-scatter.1
  343.5 254.9 all-reduce.5
  601.8 83.7 all-reduce.3
where the time goes:
time: 701 us; the launch traced here: 696 us
  waiting for transfers between devices  501 us (71%)
  blocking collectives  74.9 us (11%)
  matrix products  65.5 us (9%)
  other arithmetic  23.1 us (3%)
  local copies, waits for them, and re-layouts  16.4 us (2%)
  between operations  13.9 us (2%)
    psum x1, waiting for transfers between devices, body(): grad_w_in, grad_w_out = lax.psum((grad_w_in, grad_w_out), ('item', 'user'))  254 us
    reduce_scatter x1, waiting for transfers between devices, body(): lax.psum_scatter(item_terms.reshape(shard_rows, width), 'user', scatter_d...  129 us
    psum x1, waiting for transfers between devices, body(): grad_user = lax.psum(user_part, 'item')  85 us
    all_gather x1, blocking collectives, body(): lax.all_gather(valid, 'user', axis=0, tiled=True)  39 us
    all_gather x1, waiting for transfers between devices, body(): lax.all_gather(item_vec, 'user', axis=0, tiled=True)  31.8 us
    dot_general x16, matrix products, block_terms(): scores = jnp.dot(users, vec_block.T, preferred_element_type=jnp.float32)  31.4 us
    pmax x1, blocking collectives, body(): row_peak = lax.pmax(part_peak, 'item')  20.3 us
    psum x1, blocking collectives, body(): row_total = lax.psum(part_total * jnp.exp(part_peak - row_peak), 'item')  15.6 us
  transfers between devices with their start and end apart: 4, of which 4 were waited for; matrix products, arithmetic and copies ran while one was open for 0% of the time, Pallas kernels for 0%

commit v1 on v0

v1 whole, which is shorter than its diff:
```python
import functools

import jax
import jax.numpy as jnp
from jax import lax
from jax.experimental import pallas as pl
from jax.experimental.pallas import tpu as pltpu
from jax.sharding import PartitionSpec as P

MESH = pl.DeviceIdType.MESH
F32 = jnp.float32
BF16 = jnp.bfloat16
DEAD = -1e30
FLOOR = -1e29


def dot(a, b):
    return jnp.dot(a, b, preferred_element_type=F32)


def dot_t(a, b):
    return lax.dot_general(a, b, (((1,), (1,)), ((), ())), preferred_element_type=F32)


class Dims:
    def __init__(self, phys, ub, ib, emb, hid):
        self.ny, self.nxh, self.nxl, self.nz, self.nc = phys
        self.ub, self.ib, self.emb, self.hid = ub, ib, emb, hid
        self.ng = self.ny * self.nxh
        self.np = self.ng * self.nxl
        self.nq = self.nz * self.nc
        self.nj = self.nxl * self.nc
        self.users = self.nz * ub
        self.items = self.nj * ib
        self.wrows = 2 * emb // self.np
        self.lanes = min(self.nq, hid // 128)
        self.prow = self.wrows // (self.nq // self.lanes)
        self.pcol = hid // self.lanes


def kernel(
    d,
    users_in, weight_in, pos_in, feats, valid_in, w_in, w_out,
    out_user, out_item, out_w_in, out_w_out,
    users, meta, vecs, valid, vcol, vec_t, hidden, slope, expo, grad,
    peak_s, total_s, factor, pos_s, weight_s,
    st_own, st_a, st_own2, st_b,
    gv_send, gv_recv, gv_own, gu_send, gu_recv, gu_sum, gu2_recv, gu_out,
    wg_own, wg_send, wg_recv, p2_own, p2_recv, a2, a1,
    us_s, us_r, me_s, me_r, ve_s, ve_r, va_s, va_r, sa_s, sa_r, sb_s, sb_r,
    gv_s, gv_r, gu_s, gu_r, g2_s, g2_r, g3_s, g3_r,
    w1_s, w1_r, w2_s, w2_r, w3_s, w3_r, w4_s, w4_r,
):
    ub, ib, emb, hid = d.ub, d.ib, d.emb, d.hid
    item = lax.axis_index("item")
    user = lax.axis_index("user")
    core = lax.rem(user, d.nc)
    z = lax.rem(user // d.nc, d.nz)
    xl = user // (d.nc * d.nz)
    plane = item * d.nxl + xl
    column = z * d.nc + core

    def dev(item_, xl_, z_, core_):
        return (item_, (xl_ * d.nz + z_) * d.nc + core_)

    def z_peer(k):
        return lax.rem(z + k, d.nz)

    def plane_peer(k):
        return lax.rem(plane + k, d.np)

    def plane_dev(p):
        return dev(p // d.nxl, lax.rem(p, d.nxl), z, core)

    def column_peer(k):
        return lax.rem(column + k, d.nq)

    def column_dev(q):
        return dev(item, xl, q // d.nc, lax.rem(q, d.nc))

    def group_peer(k):
        return lax.rem(item + k, d.ng)

    def block_dev(j):
        return dev(item, lax.rem(xl + j // d.nc, d.nxl), z, lax.rem(core + j % d.nc, d.nc))

    def remote(src, dst, send, recv, to):
        return pltpu.make_async_remote_copy(
            src_ref=src, dst_ref=dst, send_sem=send, recv_sem=recv, device_id=to, device_id_type=MESH
        )

    def each(n, fn):
        def step(k, carry):
            fn(k)
            return carry

        lax.fori_loop(1, n, step, 0)

    barrier = pltpu.get_barrier_semaphore()

    def greet(to):
        pl.semaphore_signal(barrier, inc=1, device_id=to, device_id_type=MESH)

    each(d.np, lambda k: greet(plane_dev(plane_peer(k))))
    each(d.nq, lambda k: greet(column_dev(column_peer(k))))
    diagonal = [j for j in range(d.nj) if j // d.nc and j % d.nc]
    for j in diagonal:
        greet(block_dev(j))

    users[z] = users_in[...]
    meta[z] = jnp.concatenate([pos_in[...].astype(F32), weight_in[...].astype(F32)], axis=0)
    valid[0] = valid_in[...].astype(F32)
    pl.semaphore_wait(barrier, d.np - 1 + d.nq - 1 + len(diagonal))

    def users_copy(k, slot):
        return remote(users.at[slot], users.at[slot], us_s.at[k], us_r.at[k], dev(item, xl, z_peer(k), core))

    def meta_copy(k, slot):
        return remote(meta.at[slot], meta.at[slot], me_s.at[k], me_r.at[k], dev(item, xl, z_peer(k), core))

    def send_users(k):
        users_copy(k, z).start()
        meta_copy(k, z).start()

    each(d.nz, send_users)

    def vecs_copy(j):
        return remote(vecs.at[0], vecs.at[j], ve_s.at[j], ve_r.at[j], block_dev(j))

    def valid_copy(j):
        return remote(valid.at[0], valid.at[j], va_s.at[j], va_r.at[j], block_dev(j))

    rt = min(128, ib)

    def tower(t, carry):
        rows = pl.ds(pl.multiple_of(t * rt, rt), rt)
        x = feats[rows, :]
        pre = dot(x, w_in[...])
        sigma = jax.nn.sigmoid(pre)
        hid_t = (pre * sigma).astype(BF16)
        hidden[rows, :] = hid_t
        slope[rows, :] = sigma * (1.0 + pre * (1.0 - sigma))
        vecs[0, rows, :] = (x.astype(F32) + dot(hid_t, w_out[...])).astype(BF16)
        return carry

    lax.fori_loop(0, ib // rt, tower, 0)
    for j in range(1, d.nj):
        vecs_copy(j).start()
        valid_copy(j).start()

    def local_pos(pos):
        block = pos // ib
        p_core = lax.rem(block, d.nc)
        p_z = lax.rem(block // d.nc, d.nz)
        p_xl = lax.rem(block // (d.nc * d.nz), d.nxl)
        p_item = block // (d.nc * d.nz * d.nxl)
        j = lax.rem(p_xl + d.nxl - xl, d.nxl) * d.nc + lax.rem(p_core + d.nc - core, d.nc)
        here = (p_item == item) & (p_z == z)
        return jnp.where(here, j * ib + lax.rem(pos, ib), -1)

    def scores(k, carry):
        slot = lax.rem(z + d.nz - k, d.nz)

        @pl.when(k > 0)
        def _():
            users_copy(k, slot).wait_recv()
            meta_copy(k, slot).wait_recv()

        pos = local_pos(meta[slot, 0:1, :].astype(jnp.int32))
        at = pl.multiple_of(slot * ub, ub)
        pos_s[:, pl.ds(at, ub)] = pos
        weight_s[:, pl.ds(at, ub)] = meta[slot, 1:2, :]
        for j in range(d.nj):

            @pl.when(k == 0)
            def _():
                if j > 0:
                    vecs_copy(j).wait_recv()
                    valid_copy(j).wait_recv()
                vcol[j] = jnp.broadcast_to(valid[j], (128, ib)).T

            s = dot_t(vecs[j], users[slot])
            for h in range(ub // 128):
                lanes = pl.ds(pl.multiple_of(at + h * 128, 128), 128)
                row = lax.broadcasted_iota(jnp.int32, (ib, 128), 0) + j * ib
                live = (vcol[j] > 0.5) | (row == pos[:, h * 128 : (h + 1) * 128])
                x = jnp.where(live, s[:, h * 128 : (h + 1) * 128], DEAD)
                peak = jnp.maximum(jnp.max(x, axis=0, keepdims=True), FLOOR)
                e = jnp.exp(x - peak)
                peak_s[j, :, lanes] = peak
                total_s[j, :, lanes] = jnp.sum(e, axis=0, keepdims=True)
                expo[pl.ds(j * ib, ib), lanes] = e
        return carry

    lax.fori_loop(0, d.nz, scores, 0)

    def merge(peaks, totals):
        peak = functools.reduce(jnp.maximum, peaks)
        total = sum(t * jnp.exp(p - peak) for p, t in zip(peaks, totals))
        return peak, total

    peak, total = merge([peak_s[j] for j in range(d.nj)], [total_s[j] for j in range(d.nj)])
    st_own[0:1, :] = peak
    st_own[1:2, :] = total

    def st_a_copy(k):
        return remote(st_own, st_a.at[k], sa_s.at[k], sa_r.at[k], dev(group_peer(k), xl, z, core))

    def st_b_copy(k):
        return remote(st_own2, st_b.at[k], sb_s.at[k], sb_r.at[k], dev(item, xl, z_peer(k), core))

    each(d.ng, lambda k: st_a_copy(k).start())
    for j in range(d.nj):
        vec_t[:, j * ib : (j + 1) * ib] = vecs[j].astype(F32).T.astype(BF16)
    each(d.ng, lambda k: st_a_copy(k).wait_recv())
    peak, total = merge(
        [st_own[0:1, :]] + [st_a[k, 0:1, :] for k in range(1, d.ng)],
        [st_own[1:2, :]] + [st_a[k, 1:2, :] for k in range(1, d.ng)],
    )
    st_own2[0:1, :] = peak
    st_own2[1:2, :] = total
    each(d.nz, lambda k: st_b_copy(k).start())
    each(d.nz, lambda k: st_b_copy(k).wait_recv())
    peak, total = merge(
        [st_own2[0:1, :]] + [st_b[k, 0:1, :] for k in range(1, d.nz)],
        [st_own2[1:2, :]] + [st_b[k, 1:2, :] for k in range(1, d.nz)],
    )
    scale = weight_s[...] / total
    for j in range(d.nj):
        factor[j] = scale * jnp.exp(peak_s[j] - peak)

    def gv_copy(j):
        return remote(gv_send.at[j], gv_recv.at[j], gv_s.at[j], gv_r.at[j], block_dev(j))

    for j in reversed(range(d.nj)):

        def grads(t, carry):
            rows = pl.ds(pl.multiple_of(j * ib + t * rt, rt), rt)
            row = lax.broadcasted_iota(jnp.int32, (rt, d.users), 0) + (j * ib + t * rt)
            hit = jnp.where(row == pos_s[...], weight_s[...], 0.0)
            g = (expo[rows, :] * factor[j] - hit).astype(BF16)
            grad[rows, :] = g
            acc = dot(g, users[...].reshape(d.users, emb))
            here = pl.ds(pl.multiple_of(t * rt, rt), rt)
            if j == 0:
                gv_own[here, :] = acc
            else:
                gv_send[j, here, :] = acc.astype(BF16)
            return carry

        lax.fori_loop(0, ib // rt, grads, 0)
        if j > 0:
            gv_copy(j).start()

    def gu_copy(k):
        return remote(gu_send.at[k], gu_recv.at[k], gu_s.at[k], gu_r.at[k], dev(item, xl, z_peer(k), core))

    def user_terms(slot):
        lanes = pl.ds(pl.multiple_of(slot * ub, ub), ub)
        return dot(vec_t[...], grad[:, lanes]).T

    def send_terms(k):
        gu_send[k] = user_terms(z_peer(k)).astype(BF16)
        gu_copy(k).start()

    each(d.nz, send_terms)
    gu_sum[...] = user_terms(z)

    gv = gv_own[...]
    for j in range(1, d.nj):
        gv_copy(j).wait_recv()
        gv = gv + gv_recv[j].astype(F32)
    gv = gv.astype(BF16)
    gv_own[...] = gv.astype(F32)
    gv_t = gv_own[...].T.astype(BF16)
    wg_own[emb:, :] = dot(gv_t, hidden[...])

    def back(t, carry):
        rows = pl.ds(pl.multiple_of(t * rt, rt), rt)
        g = gv_own[rows, :]
        pre = (dot_t(g.astype(BF16), w_out[...]) * slope[rows, :]).astype(BF16)
        hidden[rows, :] = pre
        out_item[rows, :] = g + dot_t(pre, w_in[...])
        return carry

    lax.fori_loop(0, ib // rt, back, 0)
    wg_own[:emb, :] = dot(feats[...].astype(F32).T.astype(BF16), hidden[...])
    for p in range(d.np):
        wg_send[p] = wg_own[p * d.wrows : (p + 1) * d.wrows, :].astype(BF16)

    def w1_copy(k):
        p = plane_peer(k)
        return remote(wg_send.at[p], wg_recv.at[k], w1_s.at[k], w1_r.at[k], plane_dev(p))

    each(d.np, lambda k: w1_copy(k).start())

    def gu_add(k):
        gu_copy(k).wait_recv()
        gu_sum[...] += gu_recv[k].astype(F32)

    each(d.nz, gu_add)
    us = ub // d.ng

    def g2_copy(k):
        to = group_peer(k)
        rows = pl.ds(pl.multiple_of(to * us, us), us)
        return remote(gu_sum.at[rows, :], gu2_recv.at[k], g2_s.at[k], g2_r.at[k], dev(to, xl, z, core))

    each(d.ng, lambda k: g2_copy(k).start())

    each(d.np, lambda k: w1_copy(k).wait_recv())
    part = wg_own[pl.ds(pl.multiple_of(plane * d.wrows, d.wrows), d.wrows), :]
    for k in range(1, d.np):
        part = part + wg_recv[k].astype(F32)

    def piece(q):
        r, c = (q // d.lanes) * d.prow, (q % d.lanes) * d.pcol
        return slice(r, r + d.prow), slice(c, c + d.pcol)

    for q in range(d.nq):
        r, c = piece(q)
        p2_own[q] = part[r, c]

    def w2_copy(k):
        q = column_peer(k)
        return remote(p2_own.at[q], p2_recv.at[k], w2_s.at[k], w2_r.at[k], column_dev(q))

    each(d.nq, lambda k: w2_copy(k).start())

    def g3_copy(k, slot):
        return remote(gu_out.at[slot], gu_out.at[slot], g3_s.at[k], g3_r.at[k], dev(group_peer(k), xl, z, core))

    each(d.ng, lambda k: g2_copy(k).wait_recv())
    mine = gu_sum[pl.ds(pl.multiple_of(item * us, us), us), :]
    for k in range(1, d.ng):
        mine = mine + gu2_recv[k]
    gu_out[item] = mine
    each(d.ng, lambda k: g3_copy(k, item).start())

    each(d.nq, lambda k: w2_copy(k).wait_recv())
    own = p2_own[column]
    for k in range(1, d.nq):
        own = own + p2_recv[k]
    a2[column] = own

    def w3_copy(k, slot):
        return remote(a2.at[slot], a2.at[slot], w3_s.at[k], w3_r.at[k], column_dev(column_peer(k)))

    each(d.nq, lambda k: w3_copy(k, column).start())

    def back_by(here, k, n):
        return lax.rem(here + n - k, n)

    each(d.nq, lambda k: w3_copy(k, back_by(column, k, d.nq)).wait_recv())
    rows_of = []
    for r in range(d.nq // d.lanes):
        rows_of.append(jnp.concatenate([a2[r * d.lanes + c] for c in range(d.lanes)], axis=1))
    a1[plane] = jnp.concatenate(rows_of, axis=0).astype(BF16)

    def w4_copy(k, slot):
        return remote(a1.at[slot], a1.at[slot], w4_s.at[k], w4_r.at[k], plane_dev(plane_peer(k)))

    each(d.np, lambda k: w4_copy(k, plane).start())

    each(d.ng, lambda k: g3_copy(k, back_by(item, k, d.ng)).wait_recv())
    out_user[...] = gu_out[...].reshape(ub, emb)

    each(d.np, lambda k: w4_copy(k, back_by(plane, k, d.np)).wait_recv())
    half = d.np // 2
    out_w_in[...] = a1[:half].astype(F32).reshape(emb, hid)
    out_w_out[...] = a1[half:].astype(F32).reshape(emb, hid).T

    def sent_z(k):
        users_copy(k, z).wait_send()
        meta_copy(k, z).wait_send()
        st_b_copy(k).wait_send()
        gu_copy(k).wait_send()

    def sent_group(k):
        st_a_copy(k).wait_send()
        g2_copy(k).wait_send()
        g3_copy(k, item).wait_send()

    def sent_plane(k):
        w1_copy(k).wait_send()
        w4_copy(k, plane).wait_send()

    def sent_column(k):
        w2_copy(k).wait_send()
        w3_copy(k, column).wait_send()

    each(d.nz, sent_z)
    each(d.ng, sent_group)
    each(d.np, sent_plane)
    each(d.nq, sent_column)
    for j in range(1, d.nj):
        vecs_copy(j).wait_send()
        valid_copy(j).wait_send()
        gv_copy(j).wait_send()


def body(phys, user_vecs, row_weight, positive, item_feats, valid, w_in, w_out):
    ub, emb = user_vecs.shape
    ib, hid = item_feats.shape[0], w_in.shape[1]
    d = Dims(phys, ub, ib, emb, hid)
    vm = pltpu.VMEM
    us = ub // d.ng
    scratch = [
        vm((d.nz, ub, emb), BF16),
        vm((d.nz, 2, ub), F32),
        vm((d.nj, ib, emb), BF16),
        vm((d.nj, 1, ib), F32),
        vm((d.nj, ib, 128), F32),
        vm((emb, d.items), BF16),
        vm((ib, hid), BF16),
        vm((ib, hid), F32),
        vm((d.items, d.users), F32),
        vm((d.items, d.users), BF16),
        vm((d.nj, 1, d.users), F32),
        vm((d.nj, 1, d.users), F32),
        vm((d.nj, 1, d.users), F32),
        vm((1, d.users), jnp.int32),
        vm((1, d.users), F32),
        vm((2, d.users), F32),
        vm((d.ng, 2, d.users), F32),
        vm((2, d.users), F32),
        vm((d.nz, 2, d.users), F32),
        vm((d.nj, ib, emb), BF16),
        vm((d.nj, ib, emb), BF16),
        vm((ib, emb), F32),
        vm((d.nz, ub, emb), BF16),
        vm((d.nz, ub, emb), BF16),
        vm((ub, emb), F32),
        vm((d.ng, us, emb), F32),
        vm((d.ng, us, emb), F32),
        vm((2 * emb, hid), F32),
        vm((d.np, d.wrows, hid), BF16),
        vm((d.np, d.wrows, hid), BF16),
        vm((d.nq, d.prow, d.pcol), F32),
        vm((d.nq, d.prow, d.pcol), F32),
        vm((d.nq, d.prow, d.pcol), F32),
        vm((d.np, d.wrows, hid), BF16),
    ]
    sems = []
    for n in (d.nz, d.nz, d.nj, d.nj, d.ng, d.nz, d.nj, d.nz, d.ng, d.ng, d.np, d.nq, d.nq, d.np):
        sems += [pltpu.SemaphoreType.DMA((n,)), pltpu.SemaphoreType.DMA((n,))]
    whole = pl.BlockSpec(memory_space=pltpu.VMEM)
    return pl.pallas_call(
        functools.partial(kernel, d),
        out_shape=(
            jax.ShapeDtypeStruct((ub, emb), F32),
            jax.ShapeDtypeStruct((ib, emb), F32),
            jax.ShapeDtypeStruct((emb, hid), F32),
            jax.ShapeDtypeStruct((hid, emb), F32),
        ),
        in_specs=[whole] * 7,
        out_specs=(whole,) * 4,
        scratch_shapes=scratch + sems,
        compiler_params=pltpu.CompilerParams(
            collective_id=0, has_side_effects=True, vmem_limit_bytes=56 * 1024 * 1024
        ),
        cost_estimate=pl.CostEstimate(
            flops=6 * d.users * d.items * emb,
            bytes_accessed=4 * 1024 * 1024,
            transcendentals=d.users * d.items,
        ),
    )(
        user_vecs,
        row_weight.reshape(1, ub),
        positive.reshape(1, ub),
        item_feats,
        valid.reshape(1, ib),
        w_in,
        w_out,
    )


def build(mesh, phys):
    return jax.shard_map(
        functools.partial(body, phys),
        mesh=mesh,
        in_specs=(
            P("user", None),
            P("user"),
            P("user"),
            P(("item", "user"), None),
            P(("item", "user")),
            P(),
            P(),
        ),
        out_specs=(P("user", None), P(("item", "user"), None), P(), P()),
        check_vma=False,
    )


def solution(mesh):
    return build(mesh, (4, 2, 2, 8, 2))
```

time: 701 us -> 96.9 us (0.14)
  waiting for transfers between devices: 501 us -> 0 us
  Pallas kernels: 0 us -> 89.5 us
  blocking collectives: 74.9 us -> 0 us
  matrix products: 65.5 us -> 0 us
  other arithmetic: 23.1 us -> 0 us
  between operations: 13.9 us -> 0.66 us
  local copies, waits for them, and re-layouts: 16.4 us -> 6.53 us
    psum x2 -> x0, waiting for transfers between devices: 339 us -> none  [the longest x1 254 us: body(): grad_w_in, grad_w_out = lax.psum((grad_w_in, grad_w_out), ('item', 'user'))]
    reduce_scatter x1 -> x0, waiting for transfers between devices: 129 us -> none  [body(): lax.psum_scatter(item_terms.reshape(shard_rows, width), 'user', scatter_d...]
    pallas_call x0 -> x1, Pallas kernels: none -> 89.5 us  [body(): pl.pallas_call(functools.partial(kernel, d), out_shape=(jax.ShapeDtypeStr...]
    dot_general x38 -> x0, matrix products: 65.5 us -> none  [the longest x16 31.4 us: block_terms(): scores = jnp.dot(users, vec_block.T, preferred_element_type=jnp.float32)]
    all_gather x1 -> x0, blocking collectives: 39 us -> none  [body(): lax.all_gather(valid, 'user', axis=0, tiled=True)]
    all_gather x1 -> x0, waiting for transfers between devices: 31.8 us -> none  [body(): lax.all_gather(item_vec, 'user', axis=0, tiled=True)]
    pmax x1 -> x0, blocking collectives: 20.3 us -> none  [body(): row_peak = lax.pmax(part_peak, 'item')]
    psum x1 -> x0, blocking collectives: 15.6 us -> none  [body(): row_total = lax.psum(part_total * jnp.exp(part_peak - row_peak), 'item')]
  transfers between devices with their start and end apart: 4 -> 0, of which waited for: 4 -> 0; matrix products, arithmetic and copies ran while one was open for 0% -> 0% of each run, Pallas kernels for 0% -> 0%
where the time goes in v1:
time: 96.9 us; the launch traced here: 96.7 us
  Pallas kernels  89.5 us (92%)
  local copies, waits for them, and re-layouts  6.53 us (7%)
    pallas_call x1, Pallas kernels, body(): pl.pallas_call(functools.partial(kernel, d), out_shape=(jax.ShapeDtypeStr...  89.5 us
    unnamed x10, local copies, waits for them, and re-layouts  5.97 us

profile of v1, /device:TPU:1, one launch (start us, length us, event | category | flops | bytes accessed | tf_op | source)
XLA Modules:
  0.0 96.7 jit_solution(17216787120643654184)
XLA Ops:
  0.6 0.0 copy-start.2
  0.6 0.6 copy-done.2
  1.3 0.6 reshape.17.weight_in
  1.9 89.5 %shard_map.102 = (f32[256,128]{1,0:T(8,128)}, f32[512,128]{1,0:T(8,128)}, f32[128,1024]{1,0:T(8,128)}, f32[1024,128]{1,0:T(8,128)}) custom-call(bf16[256,128]{1,0:T(8,128)(2,1)} %users_in.1, bf16[1,256]{1,0:T(2,128)(2,1)} %reshape.17.weight_in, s32[1,256]{1,0:T(1,128)} %bitcast.3, bf16[512,128]{1,0:T(8,128)(2,1)} %feats.1, s32[1,512]{1,0:T(1,128)} %bitcast.2, ...), custom_call_target="tpu_custom_call" | custom-call | flops 3221225472 | bytes 4194304 | tf_op jit(solution)/shard_map/pallas_call | solution.py:448
  91.3 0.0 copy-start.1
  91.3 1.6 %copy.15 = f32[256,128]{1,0:T(8,128)} copy(f32[256,128]{1,0:T(8,128)} %get-tuple-element.8) | data formatting | bytes 262144
  93.0 1.7 %copy.16 = f32[512,128]{1,0:T(8,128)} copy(f32[512,128]{1,0:T(8,128)} %get-tuple-element.9) | data formatting | bytes 524288
  94.6 0.0 copy-done.1
  94.6 0.0 copy-start
  94.6 0.8 copy.17
  95.4 0.4 copy-done
  95.9 0.8 copy.18
Async XLA Ops:
  0.6 0.7 copy-start.2
  91.3 3.3 %copy-start.1 = (f32[128,1024]{1,0:T(8,128)S(1)}, f32[128,1024]{1,0:T(8,128)}, u32[]{:S(2)}) copy-start(f32[128,1024]{1,0:T(8,128)} %get-tuple-element.10) | copy-start | bytes 1572868
  94.6 1.2 %copy-start = (f32[1024,128]{1,0:T(8,128)S(1)}, f32[1024,128]{1,0:T(8,128)}, u32[]{:S(2)}) copy-start(f32[1024,128]{1,0:T(8,128)} %get-tuple-element.11) | copy-start | bytes 1572868

commit v2 on v1

v2 whole, which is shorter than its diff:
```python
import functools

import jax
import jax.numpy as jnp
from jax import lax
from jax.experimental import pallas as pl
from jax.experimental.pallas import tpu as pltpu
from jax.sharding import PartitionSpec as P

MESH = pl.DeviceIdType.MESH
F32 = jnp.float32
BF16 = jnp.bfloat16
DEAD = -1e30
FLOOR = -1e29


def dot(a, b):
    return jnp.dot(a, b, preferred_element_type=F32)


def dot_t(a, b):
    return lax.dot_general(a, b, (((1,), (1,)), ((), ())), preferred_element_type=F32)


class Dims:
    def __init__(self, phys, ub, ib, emb, hid):
        self.ny, self.nxh, self.nxl, self.nz, self.nc = phys
        self.ub, self.ib, self.emb, self.hid = ub, ib, emb, hid
        self.ng = self.ny * self.nxh
        self.np = self.ng * self.nxl
        self.nj = self.nxl * self.nc
        self.users = self.nz * ub
        self.items = self.nj * ib
        self.chunk = min(256, ib)
        self.nk = self.items // self.chunk
        self.srows = max(16, emb // self.np)
        self.scols = emb * hid // self.np // self.srows
        self.cols = hid // self.scols


def kernel(
    d,
    users_in, weight_in, pos_in, feats, valid_in, w_in, w_out,
    out_user, out_item, out_w,
    users, meta, vecs, valid, bias, vec_t, hidden, slope, expo, grad,
    peak_s, total_s, factor, tile_s, weight_s,
    st_own, st_a, st_own2, st_b,
    gv_send, gv_recv, gv_own, gu_send, gu_recv, gu_sum, gu2_recv, gu_out,
    wg_own, wc_send, wc_recv, w1_send, w1_recv, wz, a1,
    us_s, us_r, me_s, me_r, ve_s, ve_r, va_s, va_r, sa_s, sa_r, sb_s, sb_r,
    gv_s, gv_r, gu_s, gu_r, g2_s, g2_r, g3_s, g3_r,
    wc_s, wc_r, w1_s, w1_r, wz_s, wz_r, w4_s, w4_r, w5_s, w5_r,
):
    ub, ib, emb, hid = d.ub, d.ib, d.emb, d.hid
    item = lax.axis_index("item")
    user = lax.axis_index("user")
    core = lax.rem(user, d.nc)
    z = lax.rem(lax.div(user, d.nc), d.nz)
    xl = lax.div(user, d.nc * d.nz)
    plane = item * d.nxl + xl

    def dev(item_, xl_, z_, core_):
        return (item_, (xl_ * d.nz + z_) * d.nc + core_)

    def back_by(here, k, n):
        return lax.rem(here + n - k, n)

    def z_peer(k):
        return lax.rem(z + k, d.nz)

    def z_dev(k):
        return dev(item, xl, z_peer(k), core)

    def group_dev(k):
        return dev(lax.rem(item + k, d.ng), xl, z, core)

    def plane_peer(k):
        return lax.rem(plane + k, d.np)

    def plane_dev(p):
        return dev(lax.div(p, d.nxl), lax.rem(p, d.nxl), z, core)

    sibling = dev(item, xl, z, 1 - core)
    across = dev(item, 1 - xl, z, core)

    def remote(src, dst, send, recv, to):
        return pltpu.make_async_remote_copy(
            src_ref=src, dst_ref=dst, send_sem=send, recv_sem=recv, device_id=to, device_id_type=MESH
        )

    def each(n, fn):
        def step(k, carry):
            fn(k)
            return carry

        lax.fori_loop(1, n, step, 0)

    flights = {}

    def fly(name, n, copy_out, copy_in=None, start=True):
        flights[name] = [n, copy_out, copy_in or copy_out, False]
        if start:
            each(n, lambda k: copy_out(k).start())

    def land(name):
        n, _, copy_in, _ = flights[name]
        each(n, lambda k: copy_in(k).wait_recv())
        flights[name][3] = True

    def finish():
        for name, (n, copy_out, _, landed) in flights.items():
            if not landed:
                land(name)
            each(n, lambda k: copy_out(k).wait_send())

    barrier = pltpu.get_barrier_semaphore()

    def greet(to):
        pl.semaphore_signal(barrier, inc=1, device_id=to, device_id_type=MESH)

    each(d.nz, lambda k: greet(z_dev(k)))
    each(d.np, lambda k: greet(plane_dev(plane_peer(k))))
    greet(sibling)

    users[z] = users_in[...]
    pos = pos_in[...].reshape(1, ub)
    meta[z] = jnp.concatenate([pos.astype(F32), weight_in[...].reshape(1, ub).astype(F32)], axis=0)
    valid[0] = valid_in[...].reshape(1, ib).astype(F32)
    rt = min(128, ib)

    def tower(t, carry):
        rows = pl.ds(pl.multiple_of(t * rt, rt), rt)
        x = feats[rows, :]
        pre = dot(x, w_in[...])
        sigma = jax.nn.sigmoid(pre)
        hid_t = (pre * sigma).astype(BF16)
        hidden[rows, :] = hid_t
        slope[rows, :] = sigma * (1.0 + pre * (1.0 - sigma))
        vecs[0, rows, :] = (x.astype(F32) + dot(hid_t, w_out[...])).astype(BF16)
        return carry

    lax.fori_loop(0, ib // rt, tower, 0)
    pl.semaphore_wait(barrier, d.nz - 1 + d.np - 1 + 1)

    def near(step):
        half = lax.div(step + 1, 2)
        return jnp.where(lax.rem(step, 2) == 1, half, d.nz - half)

    def users_copy(k, slot):
        return remote(users.at[slot], users.at[slot], us_s.at[k], us_r.at[k], z_dev(k))

    def meta_copy(k, slot):
        return remote(meta.at[slot], meta.at[slot], me_s.at[k], me_r.at[k], z_dev(k))

    def vecs_copy(j):
        return remote(vecs.at[j // 3 * 2], vecs.at[j], ve_s.at[j], ve_r.at[j], across if j == 2 else sibling)

    def valid_copy(j):
        return remote(valid.at[j // 3 * 2], valid.at[j], va_s.at[j], va_r.at[j], across if j == 2 else sibling)

    for j in (2, 1):
        vecs_copy(j).start()
        valid_copy(j).start()
    fly("meta", d.nz, lambda k: meta_copy(near(k), z), lambda k: meta_copy(k, back_by(z, k, d.nz)))
    fly("users", d.nz, lambda k: users_copy(near(k), z), lambda k: users_copy(k, back_by(z, k, d.nz)))

    def vec_arrives(j):
        vecs_copy(j).wait_recv()
        valid_copy(j).wait_recv()

    def user_slot(step):
        return lax.rem(z + d.nz - near(step), d.nz)

    def local_tile(pos):
        block = pos // ib
        p_core = block % d.nc
        p_z = block // d.nc % d.nz
        p_xl = block // (d.nc * d.nz) % d.nxl
        p_item = block // (d.nc * d.nz * d.nxl)
        j = (p_xl + d.nxl - xl) % d.nxl * d.nc + (p_core + d.nc - core) % d.nc
        here = (p_item == item) & (p_z == z)
        row = jnp.where(here, j * ib + pos % ib, -1)
        lane = lax.broadcasted_iota(jnp.int32, (8, ub), 0)
        return jnp.where(here & (lane == row % 8), row // 8, -1)

    def set_bias(j):
        bias[j] = (jnp.broadcast_to(valid[j], (128, ib)).T - 1.0) * -DEAD

    def enter(step, slot):
        @pl.when(step > 0)
        def _():
            k = near(step)
            users_copy(k, slot).wait_recv()
            meta_copy(k, slot).wait_recv()

        lanes = pl.ds(pl.multiple_of(slot * ub, ub), ub)
        tile_s[:, lanes] = local_tile(meta[slot, 0:1, :].astype(jnp.int32))
        weight_s[:, lanes] = meta[slot, 1:2, :]

    def score(j, slot):
        at = pl.multiple_of(slot * ub, ub)
        for c in range(ib // d.chunk):
            rows = slice(c * d.chunk, (c + 1) * d.chunk)
            s = dot_t(vecs[j, rows, :], users[slot])
            b = bias[j, rows, :].reshape(d.chunk // 8, 8, 128)
            first = j * ib + c * d.chunk
            tile = lax.broadcasted_iota(jnp.int32, (d.chunk // 8, 8, 128), 0) + first // 8
            for h in range(ub // 128):
                lanes = pl.ds(pl.multiple_of(at + h * 128, 128), 128)
                sh = s[:, h * 128 : (h + 1) * 128].reshape(d.chunk // 8, 8, 128)
                x = jnp.where(tile == tile_s[:, lanes][None], sh, sh + b)
                peak = jnp.maximum(jnp.max(x, axis=0), FLOOR)
                e = jnp.exp(x - peak[None])
                ck = first // d.chunk
                peak_s[ck, :, lanes] = peak
                total_s[ck, :, lanes] = jnp.sum(e, axis=0)
                expo[pl.ds(first, d.chunk), lanes] = e.reshape(d.chunk, 128)

    def score_steps(lo, hi, blocks, arrive):
        def step(i, carry):
            slot = jnp.where(i == 0, z, user_slot(i))
            if arrive:
                enter(i, slot)
            for j in blocks:
                score(j, slot)
            return carry

        lax.fori_loop(lo, hi, step, 0)

    early = min(3, d.nz)
    set_bias(0)
    vec_arrives(1)
    set_bias(1)
    score_steps(0, early, (0, 1), True)
    vec_arrives(2)
    vecs_copy(3).start()
    valid_copy(3).start()
    set_bias(2)
    score_steps(0, early, (2,), False)
    vec_arrives(3)
    set_bias(3)
    fly("vecs", d.nj, None, start=False)
    flights.pop("vecs")
    score_steps(0, early, (3,), False)
    score_steps(early, d.nz, (0, 1, 2, 3), True)
    for name in ("users", "meta"):
        flights[name][3] = True

    def merge(peaks, totals):
        peak = functools.reduce(jnp.maximum, peaks)
        total = sum(t * jnp.exp(p - peak) for p, t in zip(peaks, totals))
        return peak, total

    peak8 = functools.reduce(jnp.maximum, [peak_s[c] for c in range(d.nk)])
    peak = jnp.max(peak8, axis=0, keepdims=True)
    total8 = sum(total_s[c] * jnp.exp(peak_s[c] - peak) for c in range(d.nk))
    st_own[0:1, :] = peak
    st_own[1:2, :] = jnp.sum(total8, axis=0, keepdims=True)

    def st_a_copy(k):
        return remote(st_own, st_a.at[k], sa_s.at[k], sa_r.at[k], group_dev(k))

    def st_b_copy(k):
        return remote(st_own2, st_b.at[k], sb_s.at[k], sb_r.at[k], z_dev(k))

    fly("st_a", d.ng, st_a_copy)
    for j in range(d.nj):
        vec_t[:, j * ib : (j + 1) * ib] = vecs[j].astype(F32).T.astype(BF16)
    land("st_a")
    peak, total = merge(
        [st_own[0:1, :]] + [st_a[k, 0:1, :] for k in range(1, d.ng)],
        [st_own[1:2, :]] + [st_a[k, 1:2, :] for k in range(1, d.ng)],
    )
    st_own2[0:1, :] = peak
    st_own2[1:2, :] = total
    fly("st_b", d.nz, st_b_copy)
    land("st_b")
    peak, total = merge(
        [st_own2[0:1, :]] + [st_b[k, 0:1, :] for k in range(1, d.nz)],
        [st_own2[1:2, :]] + [st_b[k, 1:2, :] for k in range(1, d.nz)],
    )
    scale = weight_s[...] / total
    for c in range(d.nk):
        factor[c] = scale * jnp.exp(peak_s[c] - peak)

    def grads(j):
        acc = jnp.zeros((ib, emb), F32)
        width = min(512, d.users)
        tile = lax.broadcasted_iota(jnp.int32, (ib // 8, 8, width), 0) + j * ib // 8
        per = ib // d.chunk
        for u in range(0, d.users, width):
            lanes = slice(u, u + width)
            e = expo[j * ib : (j + 1) * ib, lanes].reshape(per, d.chunk // 8, 8, width)
            e = (e * factor[j * per : (j + 1) * per, :, lanes][:, None]).reshape(ib // 8, 8, width)
            hit = tile == tile_s[:, lanes][None]
            g = jnp.where(hit, e - weight_s[:, lanes][None], e).reshape(ib, width).astype(BF16)
            grad[j * ib : (j + 1) * ib, lanes] = g
            acc = acc + dot(g, users[...].reshape(d.users, emb)[lanes, :])
        return acc

    def gv_copy(j):
        return remote(gv_send.at[j], gv_recv.at[j], gv_s.at[j], gv_r.at[j], across if j == 2 else sibling)

    gv_send[3] = grads(3).astype(BF16)
    gv_copy(3).start()
    acc = grads(2)
    gv_copy(3).wait_recv()
    gv_send[2] = (acc + gv_recv[3].astype(F32)).astype(BF16)
    gv_copy(2).start()
    gv_send[1] = grads(1).astype(BF16)
    gv_copy(1).start()
    gv_own[...] = grads(0)

    def gu_copy(k):
        return remote(gu_send.at[k], gu_recv.at[k], gu_s.at[k], gu_r.at[k], z_dev(k))

    def user_terms(slot):
        lanes = pl.ds(pl.multiple_of(slot * ub, ub), ub)
        return dot(vec_t[...], grad[:, lanes]).T

    def send_terms(step):
        k = near(d.nz - step)
        gu_send[k] = user_terms(z_peer(k)).astype(BF16)
        gu_copy(k).start()

    fly("gu", d.nz, gu_copy, start=False)
    each(d.nz, send_terms)
    gu_sum[...] = user_terms(z)

    for j in (1, 2):
        gv_copy(j).wait_recv()
    gv = gv_own[...] + gv_recv[1].astype(F32) + gv_recv[2].astype(F32)
    gv = gv.astype(BF16)
    gv_own[...] = gv.astype(F32)
    gv_t = gv_own[...].T.astype(BF16)
    wg_own[1] = dot(gv_t, hidden[...])

    def back(t, carry):
        rows = pl.ds(pl.multiple_of(t * rt, rt), rt)
        g = gv_own[rows, :]
        pre = (dot_t(g.astype(BF16), w_out[...]) * slope[rows, :]).astype(BF16)
        hidden[rows, :] = pre
        out_item[rows, :] = g + dot_t(pre, w_in[...])
        return carry

    lax.fori_loop(0, ib // rt, back, 0)
    wg_own[0] = dot(feats[...].astype(F32).T.astype(BF16), hidden[...])

    wc_send[...] = wg_own[1 - core].astype(BF16)
    wc_copy = remote(wc_send, wc_recv, wc_s, wc_r, sibling)
    wc_copy.start()
    wc_copy.wait_recv()
    wg_own[core] += wc_recv[...].astype(F32)
    sr, sc = d.srows, d.scols
    for p in range(d.np):
        r, c = p // d.cols * sr, p % d.cols * sc
        w1_send[p] = wg_own[core, r : r + sr, c : c + sc].astype(BF16)

    def w1_copy(k):
        p = plane_peer(k)
        return remote(w1_send.at[p], w1_recv.at[k], w1_s.at[k], w1_r.at[k], plane_dev(p))

    fly("w1", d.np, w1_copy)
    land("w1")
    part = w1_send[plane].astype(F32)
    for k in range(1, d.np):
        part = part + w1_recv[k].astype(F32)
    wz[z] = part.astype(BF16)

    def wz_copy(k, slot):
        return remote(wz.at[slot], wz.at[slot], wz_s.at[k], wz_r.at[k], z_dev(k))

    fly("wz", d.nz, lambda k: wz_copy(k, z), lambda k: wz_copy(k, back_by(z, k, d.nz)))

    land("gu")

    def gu_add(k):
        gu_sum[...] += gu_recv[k].astype(F32)

    each(d.nz, gu_add)
    us = ub // d.ng

    def g2_copy(k):
        to = lax.rem(item + k, d.ng)
        rows = pl.ds(pl.multiple_of(to * us, us), us)
        return remote(gu_sum.at[rows, :], gu2_recv.at[k], g2_s.at[k], g2_r.at[k], dev(to, xl, z, core))

    fly("g2", d.ng, g2_copy)
    land("wz")
    whole = sum(wz[k].astype(F32) for k in range(d.nz))
    a1[core, plane] = whole.astype(BF16)

    def w4_copy(k, slot):
        there = a1.at[core, slot]
        return remote(there, there, w4_s.at[k], w4_r.at[k], plane_dev(plane_peer(k)))

    def w5_copy(k, slot, of):
        there = a1.at[of, slot]
        return remote(there, there, w5_s.at[k], w5_r.at[k], sibling)

    fly("w4", d.np, lambda k: w4_copy(k, plane), lambda k: w4_copy(k, back_by(plane, k, d.np)))
    w5_copy(0, plane, core).start()

    land("g2")
    mine = gu_sum[pl.ds(pl.multiple_of(item * us, us), us), :]
    for k in range(1, d.ng):
        mine = mine + gu2_recv[k]
    gu_out[item] = mine

    def g3_copy(k, slot):
        return remote(gu_out.at[slot], gu_out.at[slot], g3_s.at[k], g3_r.at[k], group_dev(k))

    fly("g3", d.ng, lambda k: g3_copy(k, item), lambda k: g3_copy(k, back_by(item, k, d.ng)))

    def hand_on(k):
        slot = back_by(plane, k, d.np)
        w4_copy(k, slot).wait_recv()
        w5_copy(k, slot, core).start()

    each(d.np, hand_on)
    flights["w4"][3] = True
    land("g3")
    out_user[...] = gu_out[...].reshape(ub, emb)
    w5_copy(0, plane, 1 - core).wait_recv()
    each(d.np, lambda k: w5_copy(k, back_by(plane, k, d.np), 1 - core).wait_recv())
    out_w[...] = a1[...]

    finish()
    for j in (1, 2, 3):
        vecs_copy(j).wait_send()
        valid_copy(j).wait_send()
        gv_copy(j).wait_send()
    wc_copy.wait_send()
    w5_copy(0, plane, core).wait_send()
    each(d.np, lambda k: w5_copy(k, back_by(plane, k, d.np), core).wait_send())


def unpack(d, user_ref, item_ref, w_ref, out_user, out_item, out_w_in, out_w_out):
    out_user[...] = user_ref[...]
    out_item[...] = item_ref[...]
    for p in range(d.np):
        r, c = p // d.cols * d.srows, p % d.cols * d.scols
        out_w_in[r : r + d.srows, c : c + d.scols] = w_ref[0, p].astype(F32)
    for c in range(d.cols):
        block = jnp.concatenate([w_ref[1, p].astype(F32) for p in range(c, d.np, d.cols)], axis=0)
        out_w_out[c * d.scols : (c + 1) * d.scols, :] = block.T


def body(phys, user_vecs, row_weight, positive, item_feats, valid, w_in, w_out):
    ub, emb = user_vecs.shape
    ib, hid = item_feats.shape[0], w_in.shape[1]
    d = Dims(phys, ub, ib, emb, hid)
    vm = pltpu.VMEM
    us = ub // d.ng
    scratch = [
        vm((d.nz, ub, emb), BF16),
        vm((d.nz, 2, ub), F32),
        vm((d.nj, ib, emb), BF16),
        vm((d.nj, 1, ib), F32),
        vm((d.nj, ib, 128), F32),
        vm((emb, d.items), BF16),
        vm((ib, hid), BF16),
        vm((ib, hid), F32),
        vm((d.items, d.users), F32),
        vm((d.items, d.users), BF16),
        vm((d.nk, 8, d.users), F32),
        vm((d.nk, 8, d.users), F32),
        vm((d.nk, 8, d.users), F32),
        vm((8, d.users), jnp.int32),
        vm((1, d.users), F32),
        vm((2, d.users), F32),
        vm((d.ng, 2, d.users), F32),
        vm((2, d.users), F32),
        vm((d.nz, 2, d.users), F32),
        vm((d.nj, ib, emb), BF16),
        vm((d.nj, ib, emb), BF16),
        vm((ib, emb), F32),
        vm((d.nz, ub, emb), BF16),
        vm((d.nz, ub, emb), BF16),
        vm((ub, emb), F32),
        vm((d.ng, us, emb), F32),
        vm((d.ng, us, emb), F32),
        vm((2, emb, hid), F32),
        vm((emb, hid), BF16),
        vm((emb, hid), BF16),
        vm((d.np, d.srows, d.scols), BF16),
        vm((d.np, d.srows, d.scols), BF16),
        vm((d.nz, d.srows, d.scols), BF16),
        vm((2, d.np, d.srows, d.scols), BF16),
    ]
    dma = pltpu.SemaphoreType.DMA
    sems = []
    for n in (d.nz, d.nz, d.nj, d.nj, d.ng, d.nz, d.nj, d.nz, d.ng, d.ng, None, d.np, d.nz, d.np, d.np):
        sems += [dma, dma] if n is None else [dma((n,)), dma((n,))]
    whole = pl.BlockSpec(memory_space=pltpu.VMEM)
    parts = pl.pallas_call(
        functools.partial(kernel, d),
        out_shape=(
            jax.ShapeDtypeStruct((ub, emb), F32),
            jax.ShapeDtypeStruct((ib, emb), F32),
            jax.ShapeDtypeStruct((2, d.np, d.srows, d.scols), BF16),
        ),
        in_specs=[whole] * 7,
        out_specs=(whole,) * 3,
        scratch_shapes=scratch + sems,
        compiler_params=pltpu.CompilerParams(
            collective_id=0, has_side_effects=True, vmem_limit_bytes=56 * 1024 * 1024
        ),
        cost_estimate=pl.CostEstimate(
            flops=6 * d.users * d.items * emb,
            bytes_accessed=4 * 1024 * 1024,
            transcendentals=d.users * d.items,
        ),
    )(user_vecs, row_weight, positive, item_feats, valid, w_in, w_out)
    return pl.pallas_call(
        functools.partial(unpack, d),
        out_shape=(
            jax.ShapeDtypeStruct((ub, emb), F32),
            jax.ShapeDtypeStruct((ib, emb), F32),
            jax.ShapeDtypeStruct((emb, hid), F32),
            jax.ShapeDtypeStruct((hid, emb), F32),
        ),
        in_specs=[whole] * 3,
        out_specs=(whole,) * 4,
    )(*parts)


def build(mesh, phys):
    return jax.shard_map(
        functools.partial(body, phys),
        mesh=mesh,
        in_specs=(
            P("user", None),
            P("user"),
            P("user"),
            P(("item", "user"), None),
            P(("item", "user")),
            P(),
            P(),
        ),
        out_specs=(P("user", None), P(("item", "user"), None), P(), P()),
        check_vma=False,
    )


def solution(mesh):
    return build(mesh, (4, 2, 2, 8, 2))
```

time: 96.9 us -> 77.4 us (0.80)
  Pallas kernels: 89.5 us -> 76.6 us
  local copies, waits for them, and re-layouts: 6.53 us -> 0 us
    pallas_call x1, Pallas kernels: 89.5 us -> 74.2 us  [body(): pl.pallas_call(functools.partial(kernel, d), out_shape=(jax.ShapeDtypeStr...]
    unnamed x10 -> x0, local copies, waits for them, and re-layouts: 5.97 us -> none
    pallas_call x0 -> x1, Pallas kernels: none -> 2.36 us  [body(): pl.pallas_call(functools.partial(unpack, d), out_shape=(jax.ShapeDtypeStr...]
where the time goes in v2:
time: 77.4 us; the launch traced here: 77.2 us
  Pallas kernels  76.6 us (99%)
    pallas_call x1, Pallas kernels, body(): pl.pallas_call(functools.partial(kernel, d), out_shape=(jax.ShapeDtypeStr...  74.2 us
    pallas_call x1, Pallas kernels, body(): pl.pallas_call(functools.partial(unpack, d), out_shape=(jax.ShapeDtypeStr...  2.36 us

profile of v2, /device:TPU:1, one launch (start us, length us, event | category | flops | bytes accessed | tf_op | source)
XLA Modules:
  0.0 77.2 jit_solution(8117072794448542796)
XLA Ops:
  0.6 74.2 %shard_map.102 = (f32[256,128]{1,0:T(8,128)}, f32[512,128]{1,0:T(8,128)}, bf16[2,16,16,512]{3,2,1,0:T(8,128)(2,1)}) custom-call(bf16[256,128]{1,0:T(8,128)(2,1)} %users_in.1, bf16[256]{0:T(256)(128)(2,1)} %weight_in.1, s32[256]{0:T(256)} %pos_in.1, bf16[512,128]{1,0:T(8,128)(2,1)} %feats.1, s32[512]{0:T(512)} %valid_in.1, bf16[128,1024]{1,0:T(8,128)(2,1)} %w_in.1, ...), custom_call_target="tpu_custom_call" | custom-call | flops 3221225472 | bytes 4194304 | tf_op jit(solution)/shard_map/pallas_call | solution.py:496
  74.9 2.4 %shard_map.103 = (f32[256,128]{1,0:T(8,128)}, f32[512,128]{1,0:T(8,128)}, f32[128,1024]{1,0:T(8,128)}, f32[1024,128]{1,0:T(8,128)}) custom-call(f32[256,128]{1,0:T(8,128)} %get-tuple-element.7.user_ref, f32[512,128]{1,0:T(8,128)} %get-tuple-element.8.item_ref, bf16[2,16,16,512]{3,2,1,0:T(8,128)(2,1)} %get-tuple-element.9.w_ref), custom_call_target="tpu_custom_call" | custom-call | tf_op jit(solution)/shard_map/pallas_call | solution.py:515

commit v3 on v2

--- a/solution.py
+++ b/solution.py
@@ -33,9 +33,8 @@
         self.items = self.nj * ib
         self.chunk = min(256, ib)
         self.nk = self.items // self.chunk
-        self.srows = max(16, emb // self.np)
-        self.scols = emb * hid // self.np // self.srows
-        self.cols = hid // self.scols
+        self.srows = 2 * emb // self.np
+        self.scols = hid // 2
 
 
 def kernel(
@@ -107,7 +106,24 @@
         each(n, lambda k: copy_in(k).wait_recv())
         flights[name][3] = True
 
+    tails = []
+    singles = {}
+
+    def launch(name, make):
+        singles[name] = [make, False]
+        make().start()
+
+    def arrive(name):
+        singles[name][0]().wait_recv()
+        singles[name][1] = True
+
     def finish():
+        for wait in tails:
+            wait()
+        for make, landed in singles.values():
+            if not landed:
+                make().wait_recv()
+            make().wait_send()
         for name, (n, copy_out, _, landed) in flights.items():
             if not landed:
                 land(name)
@@ -146,11 +162,41 @@
         half = lax.div(step + 1, 2)
         return jnp.where(lax.rem(step, 2) == 1, half, d.nz - half)
 
-    def users_copy(k, slot):
-        return remote(users.at[slot], users.at[slot], us_s.at[k], us_r.at[k], z_dev(k))
-
-    def meta_copy(k, slot):
-        return remote(meta.at[slot], meta.at[slot], me_s.at[k], me_r.at[k], z_dev(k))
+    far = d.nz // 2
+
+    def users_copies(k, slot, to):
+        there = z_dev(to)
+        return [
+            remote(users.at[slot], users.at[slot], us_s.at[k], us_r.at[k], there),
+            remote(meta.at[slot], meta.at[slot], me_s.at[k], me_r.at[k], there),
+        ]
+
+    def users_start(k, slot, to):
+        for copy in users_copies(k, slot, to):
+            copy.start()
+
+    def users_sent():
+        for k in range(1, d.nz):
+            for copy in users_copies(k, z, 1):
+                copy.wait_send()
+
+    def users_arrive(k, slot):
+        for copy in users_copies(k, slot, 1):
+            copy.wait_recv()
+
+    direct = [k for k in (1, d.nz - 1, 2, d.nz - 2) if 0 < k < d.nz]
+    direct = sorted(set(direct), key=direct.index)
+    handed = [k for k in range(1, d.nz) if k not in direct]
+
+    def hand_on_users():
+        for k in handed:
+            if k < far:
+                users_start(k, back_by(z, 2, d.nz), 1)
+            elif k > far:
+                users_start(k, back_by(z, d.nz - 2, d.nz), d.nz - 1)
+            else:
+                behind = jnp.where(core == 0, 2, d.nz - 2)
+                users_start(k, back_by(z, behind, d.nz), behind)
 
     def vecs_copy(j):
         return remote(vecs.at[j // 3 * 2], vecs.at[j], ve_s.at[j], ve_r.at[j], across if j == 2 else sibling)
@@ -159,14 +205,15 @@
         return remote(valid.at[j // 3 * 2], valid.at[j], va_s.at[j], va_r.at[j], across if j == 2 else sibling)
 
     for j in (2, 1):
-        vecs_copy(j).start()
-        valid_copy(j).start()
-    fly("meta", d.nz, lambda k: meta_copy(near(k), z), lambda k: meta_copy(k, back_by(z, k, d.nz)))
-    fly("users", d.nz, lambda k: users_copy(near(k), z), lambda k: users_copy(k, back_by(z, k, d.nz)))
+        launch(f"vecs{j}", functools.partial(vecs_copy, j))
+        launch(f"valid{j}", functools.partial(valid_copy, j))
+    for k in direct:
+        users_start(k, z, k)
+    tails.append(users_sent)
 
     def vec_arrives(j):
-        vecs_copy(j).wait_recv()
-        valid_copy(j).wait_recv()
+        arrive(f"vecs{j}")
+        arrive(f"valid{j}")
 
     def user_slot(step):
         return lax.rem(z + d.nz - near(step), d.nz)
@@ -187,75 +234,95 @@
         bias[j] = (jnp.broadcast_to(valid[j], (128, ib)).T - 1.0) * -DEAD
 
     def enter(step, slot):
-        @pl.when(step > 0)
-        def _():
-            k = near(step)
-            users_copy(k, slot).wait_recv()
-            meta_copy(k, slot).wait_recv()
-
         lanes = pl.ds(pl.multiple_of(slot * ub, ub), ub)
         tile_s[:, lanes] = local_tile(meta[slot, 0:1, :].astype(jnp.int32))
         weight_s[:, lanes] = meta[slot, 1:2, :]
 
     def score(j, slot):
         at = pl.multiple_of(slot * ub, ub)
+        tile = lax.broadcasted_iota(jnp.int32, (d.chunk // 8, 8, 128), 0)
         for c in range(ib // d.chunk):
             rows = slice(c * d.chunk, (c + 1) * d.chunk)
             s = dot_t(vecs[j, rows, :], users[slot])
             b = bias[j, rows, :].reshape(d.chunk // 8, 8, 128)
-            first = j * ib + c * d.chunk
-            tile = lax.broadcasted_iota(jnp.int32, (d.chunk // 8, 8, 128), 0) + first // 8
+            ck = j * (ib // d.chunk) + c
+            first = pl.multiple_of(ck * d.chunk, d.chunk)
             for h in range(ub // 128):
                 lanes = pl.ds(pl.multiple_of(at + h * 128, 128), 128)
                 sh = s[:, h * 128 : (h + 1) * 128].reshape(d.chunk // 8, 8, 128)
-                x = jnp.where(tile == tile_s[:, lanes][None], sh, sh + b)
+                hit = tile == (tile_s[:, lanes] - ck * (d.chunk // 8))[None]
+                x = jnp.where(hit, sh, sh + b)
                 peak = jnp.maximum(jnp.max(x, axis=0), FLOOR)
                 e = jnp.exp(x - peak[None])
-                ck = first // d.chunk
                 peak_s[ck, :, lanes] = peak
                 total_s[ck, :, lanes] = jnp.sum(e, axis=0)
                 expo[pl.ds(first, d.chunk), lanes] = e.reshape(d.chunk, 128)
 
-    def score_steps(lo, hi, blocks, arrive):
-        def step(i, carry):
-            slot = jnp.where(i == 0, z, user_slot(i))
-            if arrive:
-                enter(i, slot)
-            for j in blocks:
-                score(j, slot)
-            return carry
-
-        lax.fori_loop(lo, hi, step, 0)
-
-    early = min(3, d.nz)
-    set_bias(0)
-    vec_arrives(1)
-    set_bias(1)
-    score_steps(0, early, (0, 1), True)
-    vec_arrives(2)
-    vecs_copy(3).start()
-    valid_copy(3).start()
-    set_bias(2)
-    score_steps(0, early, (2,), False)
-    vec_arrives(3)
-    set_bias(3)
-    fly("vecs", d.nj, None, start=False)
-    flights.pop("vecs")
-    score_steps(0, early, (3,), False)
-    score_steps(early, d.nz, (0, 1, 2, 3), True)
-    for name in ("users", "meta"):
-        flights[name][3] = True
-
-    def merge(peaks, totals):
-        peak = functools.reduce(jnp.maximum, peaks)
-        total = sum(t * jnp.exp(p - peak) for p, t in zip(peaks, totals))
-        return peak, total
+    first = min(5, d.nz)
+    turn = min(3, first)
+
+    def early_steps(i, carry):
+        pair = lax.div(i, first)
+        step = lax.rem(i, first)
+        slot = jnp.where(step == 0, z, user_slot(step))
+
+        @pl.when(i == 0)
+        def _():
+            vec_arrives(1)
+            set_bias(0)
+            set_bias(1)
+
+        @pl.when(i == turn)
+        def _():
+            for k in direct:
+                if k not in (1, d.nz - 1):
+                    users_arrive(k, back_by(z, k, d.nz))
+            hand_on_users()
+            vec_arrives(2)
+            launch("vecs3", functools.partial(vecs_copy, 3))
+            launch("valid3", functools.partial(valid_copy, 3))
+
+        @pl.when(i == first)
+        def _():
+            vec_arrives(3)
+            set_bias(2)
+            set_bias(3)
+
+        for k in (1, d.nz - 1)[: d.nz - 1]:
+
+            @pl.when(i == (1 if k == 1 else 2))
+            def _():
+                users_arrive(k, back_by(z, k, d.nz))
+
+        @pl.when(pair == 0)
+        def _():
+            enter(step, slot)
+
+        score(pair * 2, slot)
+        score(pair * 2 + 1, slot)
+        return carry
+
+    lax.fori_loop(0, 2 * first, early_steps, 0)
+
+    def late_steps(step, carry):
+        k = near(step)
+        slot = user_slot(step)
+        users_arrive(k, slot)
+        enter(step, slot)
+        for j in range(d.nj):
+            score(j, slot)
+        return carry
+
+    lax.fori_loop(first, d.nz, late_steps, 0)
+
+    def merge(logs):
+        peak = functools.reduce(jnp.maximum, logs)
+        return peak + jnp.log(sum(jnp.exp(v - peak) for v in logs))
 
     peak8 = functools.reduce(jnp.maximum, [peak_s[c] for c in range(d.nk)])
     peak = jnp.max(peak8, axis=0, keepdims=True)
     total8 = sum(total_s[c] * jnp.exp(peak_s[c] - peak) for c in range(d.nk))
-    st_own[0:1, :] = peak
-    st_own[1:2, :] = jnp.sum(total8, axis=0, keepdims=True)
+    st_own[...] = peak + jnp.log(jnp.maximum(jnp.sum(total8, axis=0, keepdims=True), 1e-30))
 
     def st_a_copy(k):
         return remote(st_own, st_a.at[k], sa_s.at[k], sa_r.at[k], group_dev(k))
@@ -267,73 +334,84 @@
     for j in range(d.nj):
         vec_t[:, j * ib : (j + 1) * ib] = vecs[j].astype(F32).T.astype(BF16)
     land("st_a")
-    peak, total = merge(
-        [st_own[0:1, :]] + [st_a[k, 0:1, :] for k in range(1, d.ng)],
-        [st_own[1:2, :]] + [st_a[k, 1:2, :] for k in range(1, d.ng)],
-    )
-    st_own2[0:1, :] = peak
-    st_own2[1:2, :] = total
+    st_own2[...] = merge([st_own[...]] + [st_a[k] for k in range(1, d.ng)])
     fly("st_b", d.nz, st_b_copy)
     land("st_b")
-    peak, total = merge(
-        [st_own2[0:1, :]] + [st_b[k, 0:1, :] for k in range(1, d.nz)],
-        [st_own2[1:2, :]] + [st_b[k, 1:2, :] for k in range(1, d.nz)],
-    )
-    scale = weight_s[...] / total
+    log_total = merge([st_own2[...]] + [st_b[k] for k in range(1, d.nz)])
     for c in range(d.nk):
-        factor[c] = scale * jnp.exp(peak_s[c] - peak)
-
-    def grads(j):
+        factor[c] = weight_s[...] * jnp.exp(peak_s[c] - log_total)
+
+    def gv_copy(j):
+        return remote(gv_send.at[j], gv_recv.at[j], gv_s.at[j], gv_r.at[j], across if j == 2 else sibling)
+
+    width = min(512, d.users)
+    per = ib // d.chunk
+
+    def grads(t, carry):
+        j = jnp.where(t == 0, 3, jnp.where(t == 3, 0, t))
+        rows = pl.ds(pl.multiple_of(j * ib, ib), ib)
         acc = jnp.zeros((ib, emb), F32)
-        width = min(512, d.users)
-        tile = lax.broadcasted_iota(jnp.int32, (ib // 8, 8, width), 0) + j * ib // 8
-        per = ib // d.chunk
+        tile = lax.broadcasted_iota(jnp.int32, (ib // 8, 8, width), 0)
         for u in range(0, d.users, width):
             lanes = slice(u, u + width)
-            e = expo[j * ib : (j + 1) * ib, lanes].reshape(per, d.chunk // 8, 8, width)
-            e = (e * factor[j * per : (j + 1) * per, :, lanes][:, None]).reshape(ib // 8, 8, width)
-            hit = tile == tile_s[:, lanes][None]
+            e = expo[rows, lanes].reshape(per, d.chunk // 8, 8, width)
+            e = (e * factor[pl.ds(j * per, per), :, lanes][:, None]).reshape(ib // 8, 8, width)
+            hit = tile == (tile_s[:, lanes] - j * (ib // 8))[None]
             g = jnp.where(hit, e - weight_s[:, lanes][None], e).reshape(ib, width).astype(BF16)
-            grad[j * ib : (j + 1) * ib, lanes] = g
+            grad[rows, lanes] = g
             acc = acc + dot(g, users[...].reshape(d.users, emb)[lanes, :])
-        return acc
-
-    def gv_copy(j):
-        return remote(gv_send.at[j], gv_recv.at[j], gv_s.at[j], gv_r.at[j], across if j == 2 else sibling)
-
-    gv_send[3] = grads(3).astype(BF16)
-    gv_copy(3).start()
-    acc = grads(2)
-    gv_copy(3).wait_recv()
-    gv_send[2] = (acc + gv_recv[3].astype(F32)).astype(BF16)
-    gv_copy(2).start()
-    gv_send[1] = grads(1).astype(BF16)
-    gv_copy(1).start()
-    gv_own[...] = grads(0)
+        gv_own[...] = acc
+
+        for at, i in ((0, 3), (1, 1)):
+
+            @pl.when(t == at)
+            def _():
+                gv_send[i] = gv_own[...].astype(BF16)
+                launch(f"gv{i}", functools.partial(gv_copy, i))
+
+        @pl.when(t == 2)
+        def _():
+            arrive("gv3")
+            gv_send[2] = (gv_own[...] + gv_recv[3].astype(F32)).astype(BF16)
+            launch("gv2", functools.partial(gv_copy, 2))
+
+        return carry
+
+    lax.fori_loop(0, 4, grads, 0)
+
+    us = ub // d.ng
 
     def gu_copy(k):
-        return remote(gu_send.at[k], gu_recv.at[k], gu_s.at[k], gu_r.at[k], z_dev(k))
-
-    def user_terms(slot):
-        lanes = pl.ds(pl.multiple_of(slot * ub, ub), ub)
-        return dot(vec_t[...], grad[:, lanes]).T
-
-    def send_terms(step):
-        k = near(d.nz - step)
-        gu_send[k] = user_terms(z_peer(k)).astype(BF16)
-        gu_copy(k).start()
-
-    fly("gu", d.nz, gu_copy, start=False)
-    each(d.nz, send_terms)
-    gu_sum[...] = user_terms(z)
-
-    for j in (1, 2):
-        gv_copy(j).wait_recv()
+        to = lax.rem(item + k, d.ng)
+        return remote(gu_send.at[to], gu_recv.at[k], gu_s.at[k], gu_r.at[k], dev(to, xl, z, core))
+
+    def user_terms(i, carry):
+        lanes = pl.ds(pl.multiple_of(i * width, width), width)
+        terms = dot(vec_t[...], grad[:, lanes]).T.astype(BF16)
+        for q in range(width // us):
+            at = q % d.ng
+            gu_send[at, i * (width // ub) + q // d.ng] = terms[q * us : (q + 1) * us, :]
+        return carry
+
+    lax.fori_loop(0, d.users // width, user_terms, 0)
+    fly("gu", d.ng, gu_copy)
+
+    arrive("gv1")
+    arrive("gv2")
     gv = gv_own[...] + gv_recv[1].astype(F32) + gv_recv[2].astype(F32)
     gv = gv.astype(BF16)
     gv_own[...] = gv.astype(F32)
     gv_t = gv_own[...].T.astype(BF16)
+    hc = hid // 2
+    mine = pl.ds(pl.multiple_of(core * hc, hc), hc)
+    other = pl.ds(pl.multiple_of((1 - core) * hc, hc), hc)
+
+    def wc_copy(m):
+        return remote(wc_send.at[m], wc_recv.at[m], wc_s.at[m], wc_r.at[m], sibling)
+
     wg_own[1] = dot(gv_t, hidden[...])
+    wc_send[1] = wg_own[1, :, other].astype(BF16)
+    launch("wc1", functools.partial(wc_copy, 1))
 
     def back(t, carry):
         rows = pl.ds(pl.multiple_of(t * rt, rt), rt)
@@ -345,22 +423,38 @@
 
     lax.fori_loop(0, ib // rt, back, 0)
     wg_own[0] = dot(feats[...].astype(F32).T.astype(BF16), hidden[...])
-
-    wc_send[...] = wg_own[1 - core].astype(BF16)
-    wc_copy = remote(wc_send, wc_recv, wc_s, wc_r, sibling)
-    wc_copy.start()
-    wc_copy.wait_recv()
-    wg_own[core] += wc_recv[...].astype(F32)
-    sr, sc = d.srows, d.scols
-    for p in range(d.np):
-        r, c = p // d.cols * sr, p % d.cols * sc
-        w1_send[p] = wg_own[core, r : r + sr, c : c + sc].astype(BF16)
+    wc_send[0] = wg_own[0, :, other].astype(BF16)
+    launch("wc0", functools.partial(wc_copy, 0))
+
+    half = d.np // 2
+    sr = d.srows
 
     def w1_copy(k):
         p = plane_peer(k)
         return remote(w1_send.at[p], w1_recv.at[k], w1_s.at[k], w1_r.at[k], plane_dev(p))
 
-    fly("w1", d.np, w1_copy)
+    fly("w1", d.np, w1_copy, start=False)
+    for m in (1, 0):
+        arrive(f"wc{m}")
+        total = wg_own[m, :, mine] + wc_recv[m].astype(F32)
+        w1_send[m * half : (m + 1) * half] = total.astype(BF16).reshape(half, sr, hc)
+
+        def send(k):
+            p = plane_peer(k)
+
+            @pl.when(p < half if m == 0 else p >= half)
+            def _():
+                w1_copy(k).start()
+
+        each(d.np, send)
+
+    land("gu")
+    gu_sum[...] = gu_send[item].astype(F32) + sum(gu_recv[k].astype(F32) for k in range(1, d.ng))
+
+    def g2_copy(k):
+        return remote(gu_sum.at[z_peer(k)], gu2_recv.at[k], g2_s.at[k], g2_r.at[k], z_dev(k))
+
+    fly("g2", d.nz, g2_copy)
     land("w1")
     part = w1_send[plane].astype(F32)
     for k in range(1, d.np):
@@ -372,20 +466,17 @@
 
     fly("wz", d.nz, lambda k: wz_copy(k, z), lambda k: wz_copy(k, back_by(z, k, d.nz)))
 
-    land("gu")
-
-    def gu_add(k):
-        gu_sum[...] += gu_recv[k].astype(F32)
-
-    each(d.nz, gu_add)
-    us = ub // d.ng
-
-    def g2_copy(k):
-        to = lax.rem(item + k, d.ng)
-        rows = pl.ds(pl.multiple_of(to * us, us), us)
-        return remote(gu_sum.at[rows, :], gu2_recv.at[k], g2_s.at[k], g2_r.at[k], dev(to, xl, z, core))
-
-    fly("g2", d.ng, g2_copy)
+    land("g2")
+    mine = gu_sum[z]
+    for k in range(1, d.nz):
+        mine = mine + gu2_recv[k]
+    gu_out[item] = mine
+
+    def g3_copy(k, slot):
+        return remote(gu_out.at[slot], gu_out.at[slot], g3_s.at[k], g3_r.at[k], group_dev(k))
+
+    fly("g3", d.ng, lambda k: g3_copy(k, item), lambda k: g3_copy(k, back_by(item, k, d.ng)))
+
     land("wz")
     whole = sum(wz[k].astype(F32) for k in range(d.nz))
     a1[core, plane] = whole.astype(BF16)
@@ -400,17 +491,6 @@
 
     fly("w4", d.np, lambda k: w4_copy(k, plane), lambda k: w4_copy(k, back_by(plane, k, d.np)))
     w5_copy(0, plane, core).start()
-
-    land("g2")
-    mine = gu_sum[pl.ds(pl.multiple_of(item * us, us), us), :]
-    for k in range(1, d.ng):
-        mine = mine + gu2_recv[k]
-    gu_out[item] = mine
-
-    def g3_copy(k, slot):
-        return remote(gu_out.at[slot], gu_out.at[slot], g3_s.at[k], g3_r.at[k], group_dev(k))
-
-    fly("g3", d.ng, lambda k: g3_copy(k, item), lambda k: g3_copy(k, back_by(item, k, d.ng)))
 
     def hand_on(k):
         slot = back_by(plane, k, d.np)
@@ -426,11 +506,6 @@
     out_w[...] = a1[...]
 
     finish()
-    for j in (1, 2, 3):
-        vecs_copy(j).wait_send()
-        valid_copy(j).wait_send()
-        gv_copy(j).wait_send()
-    wc_copy.wait_send()
     w5_copy(0, plane, core).wait_send()
     each(d.np, lambda k: w5_copy(k, back_by(plane, k, d.np), core).wait_send())
 
@@ -438,12 +513,11 @@
 def unpack(d, user_ref, item_ref, w_ref, out_user, out_item, out_w_in, out_w_out):
     out_user[...] = user_ref[...]
     out_item[...] = item_ref[...]
-    for p in range(d.np):
-        r, c = p // d.cols * d.srows, p % d.cols * d.scols
-        out_w_in[r : r + d.srows, c : c + d.scols] = w_ref[0, p].astype(F32)
-    for c in range(d.cols):
-        block = jnp.concatenate([w_ref[1, p].astype(F32) for p in range(c, d.np, d.cols)], axis=0)
-        out_w_out[c * d.scols : (c + 1) * d.scols, :] = block.T
+    half = d.np // 2
+    for c in range(2):
+        cols = slice(c * d.scols, (c + 1) * d.scols)
+        out_w_in[:, cols] = w_ref[c, :half].astype(F32).reshape(d.emb, d.scols)
+        out_w_out[cols, :] = w_ref[c, half:].astype(F32).reshape(d.emb, d.scols).T
 
 
 def body(phys, user_vecs, row_weight, positive, item_feats, valid, w_in, w_out):
@@ -468,21 +542,21 @@
         vm((d.nk, 8, d.users), F32),
         vm((8, d.users), jnp.int32),
         vm((1, d.users), F32),
-        vm((2, d.users), F32),
-        vm((d.ng, 2, d.users), F32),
-        vm((2, d.users), F32),
-        vm((d.nz, 2, d.users), F32),
+        vm((1, d.users), F32),
+        vm((d.ng, 1, d.users), F32),
+        vm((1, d.users), F32),
+        vm((d.nz, 1, d.users), F32),
         vm((d.nj, ib, emb), BF16),
         vm((d.nj, ib, emb), BF16),
         vm((ib, emb), F32),
-        vm((d.nz, ub, emb), BF16),
-        vm((d.nz, ub, emb), BF16),
-        vm((ub, emb), F32),
-        vm((d.ng, us, emb), F32),
+        vm((d.ng, d.nz, us, emb), BF16),
+        vm((d.ng, d.nz, us, emb), BF16),
+        vm((d.nz, us, emb), F32),
+        vm((d.nz, us, emb), F32),
         vm((d.ng, us, emb), F32),
         vm((2, emb, hid), F32),
-        vm((emb, hid), BF16),
-        vm((emb, hid), BF16),
+        vm((2, emb, hid // 2), BF16),
+        vm((2, emb, hid // 2), BF16),
         vm((d.np, d.srows, d.scols), BF16),
         vm((d.np, d.srows, d.scols), BF16),
         vm((d.nz, d.srows, d.scols), BF16),
@@ -490,8 +564,8 @@
     ]
     dma = pltpu.SemaphoreType.DMA
     sems = []
-    for n in (d.nz, d.nz, d.nj, d.nj, d.ng, d.nz, d.nj, d.nz, d.ng, d.ng, None, d.np, d.nz, d.np, d.np):
-        sems += [dma, dma] if n is None else [dma((n,)), dma((n,))]
+    for n in (d.nz, d.nz, d.nj, d.nj, d.ng, d.nz, d.nj, d.ng, d.nz, d.ng, 2, d.np, d.nz, d.np, d.np):
+        sems += [dma((n,)), dma((n,))]
     whole = pl.BlockSpec(memory_space=pltpu.VMEM)
     parts = pl.pallas_call(
         functools.partial(kernel, d),
@@ -504,7 +578,7 @@
         out_specs=(whole,) * 3,
         scratch_shapes=scratch + sems,
         compiler_params=pltpu.CompilerParams(
-            collective_id=0, has_side_effects=True, vmem_limit_bytes=56 * 1024 * 1024
+            collective_id=0, has_side_effects=True, vmem_limit_bytes=44 * 1024 * 1024
         ),
         cost_estimate=pl.CostEstimate(
             flops=6 * d.users * d.items * emb,

time: 77.4 us -> 78 us (level)
  local copies, waits for them, and re-layouts: 0 us -> 7.79 us
  Pallas kernels: 76.6 us -> 69.2 us
    unnamed x0 -> x20, local copies, waits for them, and re-layouts: none -> 7.79 us
    pallas_call x1, Pallas kernels: 74.2 us -> 66.9 us  [body(): pl.pallas_call(functools.partial(kernel, d), out_shape=(jax.ShapeDtypeStr...]
where the time goes in v3:
time: 78 us; the launch traced here: 77.7 us
  Pallas kernels  69.2 us (89%)
  local copies, waits for them, and re-layouts  7.79 us (10%)
    pallas_call x1, Pallas kernels, body(): pl.pallas_call(functools.partial(kernel, d), out_shape=(jax.ShapeDtypeStr...  66.9 us
    unnamed x20, local copies, waits for them, and re-layouts  7.79 us
    pallas_call x1, Pallas kernels, body(): pl.pallas_call(functools.partial(unpack, d), out_shape=(jax.ShapeDtypeStr...  2.36 us

profile of v3, /device:TPU:1, one launch (start us, length us, event | category | flops | bytes accessed | tf_op | source)
XLA Modules:
  0.0 77.7 jit_solution(595186036063985175)
XLA Ops:
  0.6 0.0 copy-start.3
  0.6 0.9 %copy-done.3 = bf16[128,1024]{1,0:T(8,128)(2,1)S(1)} copy-done((bf16[128,1024]{1,0:T(8,128)(2,1)S(1)}, bf16[128,1024]{1,0:T(8,128)(2,1)}, u32[]{:S(2)}) %copy-start.3) | copy-done | bytes 262168
  1.6 0.0 copy-start.4
  1.6 0.9 %copy-done.4 = bf16[1024,128]{1,0:T(8,128)(2,1)S(1)} copy-done((bf16[1024,128]{1,0:T(8,128)(2,1)S(1)}, bf16[1024,128]{1,0:T(8,128)(2,1)}, u32[]{:S(2)}) %copy-start.4) | copy-done | bytes 262168
  2.5 0.0 copy-start.5
  2.5 0.9 %copy-done.5 = bf16[512,128]{1,0:T(8,128)(2,1)S(1)} copy-done((bf16[512,128]{1,0:T(8,128)(2,1)S(1)}, bf16[512,128]{1,0:T(8,128)(2,1)}, u32[]{:S(2)}) %copy-start.5) | copy-done | bytes 131096
  3.4 0.0 copy-start.6
  3.4 0.8 %copy-done.6 = bf16[256,128]{1,0:T(8,128)(2,1)S(1)} copy-done((bf16[256,128]{1,0:T(8,128)(2,1)S(1)}, bf16[256,128]{1,0:T(8,128)(2,1)}, u32[]{:S(2)}) %copy-start.6) | copy-done | bytes 65560
  4.3 0.0 copy-start.7
  4.3 0.7 copy-done.7
  5.0 0.0 copy-start.8
  5.0 0.7 copy-done.8
  5.6 0.0 copy-start.9
  5.6 0.7 copy-done.9
  6.3 66.9 %shard_map.102 = (f32[256,128]{1,0:T(8,128)S(1)}, f32[512,128]{1,0:T(8,128)S(1)}, bf16[2,16,16,512]{3,2,1,0:T(8,128)(2,1)S(1)}) custom-call(bf16[256,128]{1,0:T(8,128)(2,1)S(1)} %copy-done.6, bf16[256]{0:T(256)(128)(2,1)S(1)} %copy-done.9, s32[256]{0:T(256)S(1)} %copy-done.8, bf16[512,128]{1,0:T(8,128)(2,1)S(1)} %copy-done.5, s32[512]{0:T(512)S(1)} %copy-done.7, ...), custom_call_target="tpu_custom_call" | custom-call | flops 3221225472 | bytes 4194304 | tf_op jit(solution)/shard_map/pallas_call | solution.py:570
  73.2 0.0 copy-start
  73.2 0.8 %copy-done = bf16[2,16,16,512]{3,2,1,0:T(8,128)(2,1)} copy-done((bf16[2,16,16,512]{3,2,1,0:T(8,128)(2,1)}, bf16[2,16,16,512]{3,2,1,0:T(8,128)(2,1)S(1)}, u32[]{:S(2)}) %copy-start) | copy-done | bytes 524312
  74.0 0.0 copy-start.1
  74.0 0.7 copy-done.1
  74.7 0.0 copy-start.2
  74.7 0.7 copy-done.2
  75.3 2.4 %shard_map.103 = (f32[256,128]{1,0:T(8,128)}, f32[512,128]{1,0:T(8,128)}, f32[128,1024]{1,0:T(8,128)}, f32[1024,128]{1,0:T(8,128)}) custom-call(f32[256,128]{1,0:T(8,128)} %copy-done.2, f32[512,128]{1,0:T(8,128)} %copy-done.1, bf16[2,16,16,512]{3,2,1,0:T(8,128)(2,1)} %copy-done), custom_call_target="tpu_custom_call" | custom-call | tf_op jit(solution)/shard_map/pallas_call | solution.py:589
Async XLA Ops:
  0.6 1.0 %copy-start.3 = (bf16[128,1024]{1,0:T(8,128)(2,1)S(1)}, bf16[128,1024]{1,0:T(8,128)(2,1)}, u32[]{:S(2)}) copy-start(bf16[128,1024]{1,0:T(8,128)(2,1)} %w_in.1) | copy-start | bytes 786436
  1.6 0.9 %copy-start.4 = (bf16[1024,128]{1,0:T(8,128)(2,1)S(1)}, bf16[1024,128]{1,0:T(8,128)(2,1)}, u32[]{:S(2)}) copy-start(bf16[1024,128]{1,0:T(8,128)(2,1)} %w_out.1) | copy-start | bytes 786436
  2.5 0.9 %copy-start.5 = (bf16[512,128]{1,0:T(8,128)(2,1)S(1)}, bf16[512,128]{1,0:T(8,128)(2,1)}, u32[]{:S(2)}) copy-start(bf16[512,128]{1,0:T(8,128)(2,1)} %feats.1) | copy-start | bytes 393220
  3.4 0.8 %copy-start.6 = (bf16[256,128]{1,0:T(8,128)(2,1)S(1)}, bf16[256,128]{1,0:T(8,128)(2,1)}, u32[]{:S(2)}) copy-start(bf16[256,128]{1,0:T(8,128)(2,1)} %users_in.1) | copy-start | bytes 196612
  4.3 0.7 copy-start.7
  5.0 0.7 copy-start.8
  5.6 0.7 copy-start.9
  73.2 0.8 %copy-start = (bf16[2,16,16,512]{3,2,1,0:T(8,128)(2,1)}, bf16[2,16,16,512]{3,2,1,0:T(8,128)(2,1)S(1)}, u32[]{:S(2)}) copy-start(bf16[2,16,16,512]{3,2,1,0:T(8,128)(2,1)S(1)} %get-tuple-element.9.w_ref) | copy-start | bytes 1572868
  74.0 0.7 copy-start.1
  74.7 0.7 copy-start.2

commit v4 on v3

--- a/solution.py
+++ b/solution.py
@@ -151,18 +151,24 @@
         sigma = jax.nn.sigmoid(pre)
         hid_t = (pre * sigma).astype(BF16)
         hidden[rows, :] = hid_t
-        slope[rows, :] = sigma * (1.0 + pre * (1.0 - sigma))
+        slope[rows, :] = pre
         vecs[0, rows, :] = (x.astype(F32) + dot(hid_t, w_out[...])).astype(BF16)
         return carry
 
     lax.fori_loop(0, ib // rt, tower, 0)
     pl.semaphore_wait(barrier, d.nz - 1 + d.np - 1 + 1)
 
-    def near(step):
-        half = lax.div(step + 1, 2)
-        return jnp.where(lax.rem(step, 2) == 1, half, d.nz - half)
-
     far = d.nz // 2
+    direct = [k for k in (2, d.nz - 2, 1, d.nz - 1) if 0 < k < d.nz]
+    direct = sorted(set(direct), key=direct.index)
+    handed = [k for k in range(1, d.nz) if k not in direct]
+    order = [0] + direct + sorted(handed, key=lambda k: k == far)
+
+    def hops_of(step):
+        k = 0
+        for i in range(1, d.nz):
+            k = jnp.where(step == i, order[i], k)
+        return k
 
     def users_copies(k, slot, to):
         there = z_dev(to)
@@ -184,19 +190,14 @@
         for copy in users_copies(k, slot, 1):
             copy.wait_recv()
 
-    direct = [k for k in (1, d.nz - 1, 2, d.nz - 2) if 0 < k < d.nz]
-    direct = sorted(set(direct), key=direct.index)
-    handed = [k for k in range(1, d.nz) if k not in direct]
-
-    def hand_on_users():
-        for k in handed:
-            if k < far:
-                users_start(k, back_by(z, 2, d.nz), 1)
-            elif k > far:
-                users_start(k, back_by(z, d.nz - 2, d.nz), d.nz - 1)
-            else:
-                behind = jnp.where(core == 0, 2, d.nz - 2)
-                users_start(k, back_by(z, behind, d.nz), behind)
+    def hand_on_users(k):
+        slot = back_by(z, k, d.nz)
+        ahead = k == 2
+        users_start(3 if ahead else d.nz - 3, slot, 1 if ahead else d.nz - 1)
+
+        @pl.when(core == (0 if ahead else 1))
+        def _():
+            users_start(far, slot, 2 if ahead else d.nz - 2)
 
     def vecs_copy(j):
         return remote(vecs.at[j // 3 * 2], vecs.at[j], ve_s.at[j], ve_r.at[j], across if j == 2 else sibling)
@@ -216,7 +217,7 @@
         arrive(f"valid{j}")
 
     def user_slot(step):
-        return lax.rem(z + d.nz - near(step), d.nz)
+        return lax.rem(z + d.nz - hops_of(step), d.nz)
 
     def local_tile(pos):
         block = pos // ib
@@ -272,12 +273,17 @@
             set_bias(0)
             set_bias(1)
 
+        for at in range(1, first):
+
+            @pl.when(i == at)
+            def _():
+                k = order[at]
+                users_arrive(k, back_by(z, k, d.nz))
+                if handed and k in (2, d.nz - 2):
+                    hand_on_users(k)
+
         @pl.when(i == turn)
         def _():
-            for k in direct:
-                if k not in (1, d.nz - 1):
-                    users_arrive(k, back_by(z, k, d.nz))
-            hand_on_users()
             vec_arrives(2)
             launch("vecs3", functools.partial(vecs_copy, 3))
             launch("valid3", functools.partial(valid_copy, 3))
@@ -288,12 +294,6 @@
             set_bias(2)
             set_bias(3)
 
-        for k in (1, d.nz - 1)[: d.nz - 1]:
-
-            @pl.when(i == (1 if k == 1 else 2))
-            def _():
-                users_arrive(k, back_by(z, k, d.nz))
-
         @pl.when(pair == 0)
         def _():
             enter(step, slot)
@@ -305,9 +305,8 @@
     lax.fori_loop(0, 2 * first, early_steps, 0)
 
     def late_steps(step, carry):
-        k = near(step)
         slot = user_slot(step)
-        users_arrive(k, slot)
+        users_arrive(hops_of(step), slot)
         enter(step, slot)
         for j in range(d.nj):
             score(j, slot)
@@ -333,6 +332,15 @@
     fly("st_a", d.ng, st_a_copy)
     for j in range(d.nj):
         vec_t[:, j * ib : (j + 1) * ib] = vecs[j].astype(F32).T.astype(BF16)
+
+    def slopes(t, carry):
+        rows = pl.ds(pl.multiple_of(t * rt, rt), rt)
+        pre = slope[rows, :]
+        sigma = jax.nn.sigmoid(pre)
+        slope[rows, :] = sigma * (1.0 + pre * (1.0 - sigma))
+        return carry
+
+    lax.fori_loop(0, ib // rt, slopes, 0)
     land("st_a")
     st_own2[...] = merge([st_own[...]] + [st_a[k] for k in range(1, d.ng)])
     fly("st_b", d.nz, st_b_copy)
@@ -578,7 +586,7 @@
         out_specs=(whole,) * 3,
         scratch_shapes=scratch + sems,
         compiler_params=pltpu.CompilerParams(
-            collective_id=0, has_side_effects=True, vmem_limit_bytes=44 * 1024 * 1024
+            collective_id=0, has_side_effects=True, vmem_limit_bytes=56 * 1024 * 1024
         ),
         cost_estimate=pl.CostEstimate(
             flops=6 * d.users * d.items * emb,

time: 78 us -> 73.1 us (0.937)
  local copies, waits for them, and re-layouts: 7.79 us -> 0 us
  Pallas kernels: 69.2 us -> 72.4 us
    unnamed x20 -> x0, local copies, waits for them, and re-layouts: 7.79 us -> none
    pallas_call x1, Pallas kernels: 66.9 us -> 70 us  [body(): pl.pallas_call(functools.partial(kernel, d), out_shape=(jax.ShapeDtypeStr...]
where the time goes in v4:
time: 73.1 us; the launch traced here: 73 us
  Pallas kernels  72.4 us (99%)
    pallas_call x1, Pallas kernels, body(): pl.pallas_call(functools.partial(kernel, d), out_shape=(jax.ShapeDtypeStr...  70 us
    pallas_call x1, Pallas kernels, body(): pl.pallas_call(functools.partial(unpack, d), out_shape=(jax.ShapeDtypeStr...  2.36 us

profile of v4, /device:TPU:1, one launch (start us, length us, event | category | flops | bytes accessed | tf_op | source)
XLA Modules:
  0.0 73.0 jit_solution(2019391528359287832)
XLA Ops:
  0.6 70.0 %shard_map.102 = (f32[256,128]{1,0:T(8,128)}, f32[512,128]{1,0:T(8,128)}, bf16[2,16,16,512]{3,2,1,0:T(8,128)(2,1)}) custom-call(bf16[256,128]{1,0:T(8,128)(2,1)} %users_in.1, bf16[256]{0:T(256)(128)(2,1)} %weight_in.1, s32[256]{0:T(256)} %pos_in.1, bf16[512,128]{1,0:T(8,128)(2,1)} %feats.1, s32[512]{0:T(512)} %valid_in.1, bf16[128,1024]{1,0:T(8,128)(2,1)} %w_in.1, ...), custom_call_target="tpu_custom_call" | custom-call | flops 3221225472 | bytes 4194304 | tf_op jit(solution)/shard_map/pallas_call | solution.py:578
  70.7 2.4 %shard_map.103 = (f32[256,128]{1,0:T(8,128)}, f32[512,128]{1,0:T(8,128)}, f32[128,1024]{1,0:T(8,128)}, f32[1024,128]{1,0:T(8,128)}) custom-call(f32[256,128]{1,0:T(8,128)} %get-tuple-element.7.user_ref, f32[512,128]{1,0:T(8,128)} %get-tuple-element.8.item_ref, bf16[2,16,16,512]{3,2,1,0:T(8,128)(2,1)} %get-tuple-element.9.w_ref), custom_call_target="tpu_custom_call" | custom-call | tf_op jit(solution)/shard_map/pallas_call | solution.py:597

commit v5 on v4

--- a/solution.py
+++ b/solution.py
@@ -33,20 +33,20 @@
         self.items = self.nj * ib
         self.chunk = min(256, ib)
         self.nk = self.items // self.chunk
-        self.srows = 2 * emb // self.np
-        self.scols = hid // 2
+        self.srows = max(16, emb // self.np)
+        self.scols = emb * (hid // 2) // self.np // self.srows
 
 
 def kernel(
     d,
-    users_in, weight_in, pos_in, feats, valid_in, w_in, w_out,
+    users_in, weight_in, pos_in, feats_in, valid_in, w_in_in, w_out_in,
     out_user, out_item, out_w,
-    users, meta, vecs, valid, bias, vec_t, hidden, slope, expo, grad,
+    feats, w_in, w_out, users, meta, vecs, valid, bias, vec_t, hidden, slope, expo, grad,
     peak_s, total_s, factor, tile_s, weight_s,
     st_own, st_a, st_own2, st_b,
     gv_send, gv_recv, gv_own, gu_send, gu_recv, gu_sum, gu2_recv, gu_out,
     wg_own, wc_send, wc_recv, w1_send, w1_recv, wz, a1,
-    us_s, us_r, me_s, me_r, ve_s, ve_r, va_s, va_r, sa_s, sa_r, sb_s, sb_r,
+    in_s, us_s, us_r, me_s, me_r, ve_s, ve_r, va_s, va_r, sa_s, sa_r, sb_s, sb_r,
     gv_s, gv_r, gu_s, gu_r, g2_s, g2_r, g3_s, g3_r,
     wc_s, wc_r, w1_s, w1_r, wz_s, wz_r, w4_s, w4_r, w5_s, w5_r,
 ):
@@ -129,6 +129,11 @@
                 land(name)
             each(n, lambda k: copy_out(k).wait_send())
 
+    inputs = [(feats_in, feats), (w_in_in, w_in), (w_out_in, w_out), (users_in, users.at[z])]
+    inputs = [pltpu.make_async_copy(src, dst, in_s.at[i]) for i, (src, dst) in enumerate(inputs)]
+    for copy in inputs:
+        copy.start()
+
     barrier = pltpu.get_barrier_semaphore()
 
     def greet(to):
@@ -138,24 +143,17 @@
     each(d.np, lambda k: greet(plane_dev(plane_peer(k))))
     greet(sibling)
 
-    users[z] = users_in[...]
     pos = pos_in[...].reshape(1, ub)
     meta[z] = jnp.concatenate([pos.astype(F32), weight_in[...].reshape(1, ub).astype(F32)], axis=0)
     valid[0] = valid_in[...].reshape(1, ib).astype(F32)
-    rt = min(128, ib)
-
-    def tower(t, carry):
-        rows = pl.ds(pl.multiple_of(t * rt, rt), rt)
-        x = feats[rows, :]
-        pre = dot(x, w_in[...])
-        sigma = jax.nn.sigmoid(pre)
-        hid_t = (pre * sigma).astype(BF16)
-        hidden[rows, :] = hid_t
-        slope[rows, :] = pre
-        vecs[0, rows, :] = (x.astype(F32) + dot(hid_t, w_out[...])).astype(BF16)
-        return carry
-
-    lax.fori_loop(0, ib // rt, tower, 0)
+    for copy in inputs:
+        copy.wait()
+    x = feats[...]
+    pre = dot(x, w_in[...])
+    hid_t = (pre * jax.nn.sigmoid(pre)).astype(BF16)
+    hidden[...] = hid_t
+    slope[...] = pre
+    vecs[0] = (x.astype(F32) + dot(hid_t, w_out[...])).astype(BF16)
     pl.semaphore_wait(barrier, d.nz - 1 + d.np - 1 + 1)
 
     far = d.nz // 2
@@ -215,9 +213,6 @@
     def vec_arrives(j):
         arrive(f"vecs{j}")
         arrive(f"valid{j}")
-
-    def user_slot(step):
-        return lax.rem(z + d.nz - hops_of(step), d.nz)
 
     def local_tile(pos):
         block = pos // ib
@@ -234,7 +229,7 @@
     def set_bias(j):
         bias[j] = (jnp.broadcast_to(valid[j], (128, ib)).T - 1.0) * -DEAD
 
-    def enter(step, slot):
+    def enter(slot):
         lanes = pl.ds(pl.multiple_of(slot * ub, ub), ub)
         tile_s[:, lanes] = local_tile(meta[slot, 0:1, :].astype(jnp.int32))
         weight_s[:, lanes] = meta[slot, 1:2, :]
@@ -260,58 +255,56 @@
                 expo[pl.ds(first, d.chunk), lanes] = e.reshape(d.chunk, 128)
 
     first = min(5, d.nz)
-    turn = min(3, first)
+    groups = [order[1:3], order[3:5]] if d.nz >= 5 else [order[1:first]]
+    ng = len(groups)
 
     def early_steps(i, carry):
-        pair = lax.div(i, first)
-        step = lax.rem(i, first)
-        slot = jnp.where(step == 0, z, user_slot(step))
-
-        @pl.when(i == 0)
-        def _():
-            vec_arrives(1)
-            set_bias(0)
-            set_bias(1)
-
-        for at in range(1, first):
+        pair = lax.div(i, ng)
+        turn = lax.rem(i, ng)
+
+        for at, group in enumerate(groups):
 
             @pl.when(i == at)
             def _():
-                k = order[at]
-                users_arrive(k, back_by(z, k, d.nz))
-                if handed and k in (2, d.nz - 2):
-                    hand_on_users(k)
-
-        @pl.when(i == turn)
-        def _():
-            vec_arrives(2)
-            launch("vecs3", functools.partial(vecs_copy, 3))
-            launch("valid3", functools.partial(valid_copy, 3))
-
-        @pl.when(i == first)
-        def _():
-            vec_arrives(3)
-            set_bias(2)
-            set_bias(3)
-
-        @pl.when(pair == 0)
-        def _():
-            enter(step, slot)
-
-        score(pair * 2, slot)
-        score(pair * 2 + 1, slot)
+                for k in group:
+                    slot = back_by(z, k, d.nz)
+                    users_arrive(k, slot)
+                    if handed and k in (2, d.nz - 2):
+                        hand_on_users(k)
+                    enter(slot)
+
+        for q in range(len(groups[0])):
+            k = functools.reduce(lambda a, g: jnp.where(turn == g, groups[g][q], a), range(1, ng), groups[0][q])
+            slot = back_by(z, k, d.nz)
+            score(pair * 2, slot)
+            score(pair * 2 + 1, slot)
         return carry
 
-    lax.fori_loop(0, 2 * first, early_steps, 0)
-
     def late_steps(step, carry):
-        slot = user_slot(step)
-        users_arrive(hops_of(step), slot)
-        enter(step, slot)
+        k = hops_of(step)
+        slot = back_by(z, k, d.nz)
+        users_arrive(k, slot)
+        enter(slot)
         for j in range(d.nj):
             score(j, slot)
         return carry
 
+    enter(z)
+    set_bias(0)
+    score(0, z)
+    vec_arrives(1)
+    set_bias(1)
+    score(1, z)
+    lax.fori_loop(0, ng, early_steps, 0)
+    vec_arrives(2)
+    launch("vecs3", functools.partial(vecs_copy, 3))
+    launch("valid3", functools.partial(valid_copy, 3))
+    set_bias(2)
+    score(2, z)
+    vec_arrives(3)
+    set_bias(3)
+    score(3, z)
+    lax.fori_loop(ng, 2 * ng, early_steps, 0)
     lax.fori_loop(first, d.nz, late_steps, 0)
 
     def merge(logs):
@@ -333,14 +326,9 @@
     for j in range(d.nj):
         vec_t[:, j * ib : (j + 1) * ib] = vecs[j].astype(F32).T.astype(BF16)
 
-    def slopes(t, carry):
-        rows = pl.ds(pl.multiple_of(t * rt, rt), rt)
-        pre = slope[rows, :]
-        sigma = jax.nn.sigmoid(pre)
-        slope[rows, :] = sigma * (1.0 + pre * (1.0 - sigma))
-        return carry
-
-    lax.fori_loop(0, ib // rt, slopes, 0)
+    pre = slope[...]
+    sigma = jax.nn.sigmoid(pre)
+    slope[...] = sigma * (1.0 + pre * (1.0 - sigma))
     land("st_a")
     st_own2[...] = merge([st_own[...]] + [st_a[k] for k in range(1, d.ng)])
     fly("st_b", d.nz, st_b_copy)
@@ -356,7 +344,7 @@
     per = ib // d.chunk
 
     def grads(t, carry):
-        j = jnp.where(t == 0, 3, jnp.where(t == 3, 0, t))
+        j = 3 - t
         rows = pl.ds(pl.multiple_of(j * ib, ib), ib)
         acc = jnp.zeros((ib, emb), F32)
         tile = lax.broadcasted_iota(jnp.int32, (ib // 8, 8, width), 0)
@@ -370,14 +358,14 @@
             acc = acc + dot(g, users[...].reshape(d.users, emb)[lanes, :])
         gv_own[...] = acc
 
-        for at, i in ((0, 3), (1, 1)):
+        for at, i in ((0, 3), (2, 1)):
 
             @pl.when(t == at)
             def _():
                 gv_send[i] = gv_own[...].astype(BF16)
                 launch(f"gv{i}", functools.partial(gv_copy, i))
 
-        @pl.when(t == 2)
+        @pl.when(t == 1)
         def _():
             arrive("gv3")
             gv_send[2] = (gv_own[...] + gv_recv[3].astype(F32)).astype(BF16)
@@ -421,40 +409,27 @@
     wc_send[1] = wg_own[1, :, other].astype(BF16)
     launch("wc1", functools.partial(wc_copy, 1))
 
-    def back(t, carry):
-        rows = pl.ds(pl.multiple_of(t * rt, rt), rt)
-        g = gv_own[rows, :]
-        pre = (dot_t(g.astype(BF16), w_out[...]) * slope[rows, :]).astype(BF16)
-        hidden[rows, :] = pre
-        out_item[rows, :] = g + dot_t(pre, w_in[...])
-        return carry
-
-    lax.fori_loop(0, ib // rt, back, 0)
-    wg_own[0] = dot(feats[...].astype(F32).T.astype(BF16), hidden[...])
+    pre = (dot_t(gv, w_out[...]) * slope[...]).astype(BF16)
+    hidden[...] = pre
+    wg_own[0] = dot(feats[...].astype(F32).T.astype(BF16), pre)
     wc_send[0] = wg_own[0, :, other].astype(BF16)
     launch("wc0", functools.partial(wc_copy, 0))
 
-    half = d.np // 2
-    sr = d.srows
-
-    def w1_copy(k):
+    sr, sc = d.srows, d.scols
+    cols = hc // sc
+
+    def w1_copy(m, k):
         p = plane_peer(k)
-        return remote(w1_send.at[p], w1_recv.at[k], w1_s.at[k], w1_r.at[k], plane_dev(p))
-
-    fly("w1", d.np, w1_copy, start=False)
+        return remote(w1_send.at[m, p], w1_recv.at[m, k], w1_s.at[m, k], w1_r.at[m, k], plane_dev(p))
+
     for m in (1, 0):
         arrive(f"wc{m}")
-        total = wg_own[m, :, mine] + wc_recv[m].astype(F32)
-        w1_send[m * half : (m + 1) * half] = total.astype(BF16).reshape(half, sr, hc)
-
-        def send(k):
-            p = plane_peer(k)
-
-            @pl.when(p < half if m == 0 else p >= half)
-            def _():
-                w1_copy(k).start()
-
-        each(d.np, send)
+        total = (wg_own[m, :, mine] + wc_recv[m].astype(F32)).astype(BF16)
+        for c in range(cols):
+            rows = slice(c * d.np // cols, (c + 1) * d.np // cols)
+            w1_send[m, rows] = total[:, c * sc : (c + 1) * sc].reshape(d.np // cols, sr, sc)
+        fly(f"w1{m}", d.np, functools.partial(w1_copy, m))
+    out_item[...] = gv_own[...] + dot_t(hidden[...], w_in[...])
 
     land("gu")
     gu_sum[...] = gu_send[item].astype(F32) + sum(gu_recv[k].astype(F32) for k in range(1, d.ng))
@@ -463,16 +438,22 @@
         return remote(gu_sum.at[z_peer(k)], gu2_recv.at[k], g2_s.at[k], g2_r.at[k], z_dev(k))
 
     fly("g2", d.nz, g2_copy)
-    land("w1")
-    part = w1_send[plane].astype(F32)
-    for k in range(1, d.np):
-        part = part + w1_recv[k].astype(F32)
-    wz[z] = part.astype(BF16)
-
-    def wz_copy(k, slot):
-        return remote(wz.at[slot], wz.at[slot], wz_s.at[k], wz_r.at[k], z_dev(k))
-
-    fly("wz", d.nz, lambda k: wz_copy(k, z), lambda k: wz_copy(k, back_by(z, k, d.nz)))
+    def wz_copy(m, k, slot):
+        there = wz.at[m, slot]
+        return remote(there, there, wz_s.at[m, k], wz_r.at[m, k], z_dev(k))
+
+    for m in (1, 0):
+        land(f"w1{m}")
+        part = w1_send[m, plane].astype(F32)
+        for k in range(1, d.np):
+            part = part + w1_recv[m, k].astype(F32)
+        wz[m, z] = part.astype(BF16)
+        fly(
+            f"wz{m}",
+            d.nz,
+            lambda k, m=m: wz_copy(m, k, z),
+            lambda k, m=m: wz_copy(m, k, back_by(z, k, d.nz)),
+        )
 
     land("g2")
     mine = gu_sum[z]
@@ -485,47 +466,57 @@
 
     fly("g3", d.ng, lambda k: g3_copy(k, item), lambda k: g3_copy(k, back_by(item, k, d.ng)))
 
-    land("wz")
-    whole = sum(wz[k].astype(F32) for k in range(d.nz))
-    a1[core, plane] = whole.astype(BF16)
-
-    def w4_copy(k, slot):
-        there = a1.at[core, slot]
-        return remote(there, there, w4_s.at[k], w4_r.at[k], plane_dev(plane_peer(k)))
-
-    def w5_copy(k, slot, of):
-        there = a1.at[of, slot]
-        return remote(there, there, w5_s.at[k], w5_r.at[k], sibling)
-
-    fly("w4", d.np, lambda k: w4_copy(k, plane), lambda k: w4_copy(k, back_by(plane, k, d.np)))
-    w5_copy(0, plane, core).start()
-
-    def hand_on(k):
+    def w4_copy(m, k, slot):
+        there = a1.at[core, m, slot]
+        return remote(there, there, w4_s.at[m, k], w4_r.at[m, k], plane_dev(plane_peer(k)))
+
+    def w5_copy(m, k, slot, of):
+        there = a1.at[of, m, slot]
+        return remote(there, there, w5_s.at[m, k], w5_r.at[m, k], sibling)
+
+    for m in (1, 0):
+        land(f"wz{m}")
+        a1[core, m, plane] = sum(wz[m, k].astype(F32) for k in range(d.nz)).astype(BF16)
+        fly(
+            f"w4{m}",
+            d.np,
+            lambda k, m=m: w4_copy(m, k, plane),
+            lambda k, m=m: w4_copy(m, k, back_by(plane, k, d.np)),
+        )
+        w5_copy(m, 0, plane, core).start()
+
+    def hand_on(m, k):
         slot = back_by(plane, k, d.np)
-        w4_copy(k, slot).wait_recv()
-        w5_copy(k, slot, core).start()
-
-    each(d.np, hand_on)
-    flights["w4"][3] = True
+        w4_copy(m, k, slot).wait_recv()
+        w5_copy(m, k, slot, core).start()
+
+    for m in (1, 0):
+        each(d.np, functools.partial(hand_on, m))
+        flights[f"w4{m}"][3] = True
     land("g3")
     out_user[...] = gu_out[...].reshape(ub, emb)
-    w5_copy(0, plane, 1 - core).wait_recv()
-    each(d.np, lambda k: w5_copy(k, back_by(plane, k, d.np), 1 - core).wait_recv())
+    for m in (1, 0):
+        w5_copy(m, 0, plane, 1 - core).wait_recv()
+        each(d.np, lambda k: w5_copy(m, k, back_by(plane, k, d.np), 1 - core).wait_recv())
     out_w[...] = a1[...]
 
     finish()
-    w5_copy(0, plane, core).wait_send()
-    each(d.np, lambda k: w5_copy(k, back_by(plane, k, d.np), core).wait_send())
+    for m in (1, 0):
+        w5_copy(m, 0, plane, core).wait_send()
+        each(d.np, lambda k: w5_copy(m, k, back_by(plane, k, d.np), core).wait_send())
 
 
 def unpack(d, user_ref, item_ref, w_ref, out_user, out_item, out_w_in, out_w_out):
     out_user[...] = user_ref[...]
     out_item[...] = item_ref[...]
-    half = d.np // 2
-    for c in range(2):
-        cols = slice(c * d.scols, (c + 1) * d.scols)
-        out_w_in[:, cols] = w_ref[c, :half].astype(F32).reshape(d.emb, d.scols)
-        out_w_out[cols, :] = w_ref[c, half:].astype(F32).reshape(d.emb, d.scols).T
+    hc, sc = d.hid // 2, d.scols
+    cols = hc // sc
+    for half in range(2):
+        for c in range(cols):
+            parts = slice(c * d.np // cols, (c + 1) * d.np // cols)
+            at = slice(half * hc + c * sc, half * hc + (c + 1) * sc)
+            out_w_in[:, at] = w_ref[half, 0, parts].astype(F32).reshape(d.emb, sc)
+            out_w_out[at, :] = w_ref[half, 1, parts].astype(F32).reshape(d.emb, sc).T
 
 
 def body(phys, user_vecs, row_weight, positive, item_feats, valid, w_in, w_out):
@@ -535,6 +526,9 @@
     vm = pltpu.VMEM
     us = ub // d.ng
     scratch = [
+        vm((ib, emb), BF16),
+        vm((emb, hid), BF16),
+        vm((hid, emb), BF16),
         vm((d.nz, ub, emb), BF16),
         vm((d.nz, 2, ub), F32),
         vm((d.nj, ib, emb), BF16),
@@ -565,24 +559,27 @@
         vm((2, emb, hid), F32),
         vm((2, emb, hid // 2), BF16),
         vm((2, emb, hid // 2), BF16),
-        vm((d.np, d.srows, d.scols), BF16),
-        vm((d.np, d.srows, d.scols), BF16),
-        vm((d.nz, d.srows, d.scols), BF16),
         vm((2, d.np, d.srows, d.scols), BF16),
+        vm((2, d.np, d.srows, d.scols), BF16),
+        vm((2, d.nz, d.srows, d.scols), BF16),
+        vm((2, 2, d.np, d.srows, d.scols), BF16),
     ]
     dma = pltpu.SemaphoreType.DMA
-    sems = []
-    for n in (d.nz, d.nz, d.nj, d.nj, d.ng, d.nz, d.nj, d.ng, d.nz, d.ng, 2, d.np, d.nz, d.np, d.np):
+    sems = [dma((4,))]
+    for n in (d.nz, d.nz, d.nj, d.nj, d.ng, d.nz, d.nj, d.ng, d.nz, d.ng, 2):
         sems += [dma((n,)), dma((n,))]
+    for n in (d.np, d.nz, d.np, d.np):
+        sems += [dma((2, n)), dma((2, n))]
     whole = pl.BlockSpec(memory_space=pltpu.VMEM)
+    where = pl.BlockSpec(memory_space=pl.ANY)
     parts = pl.pallas_call(
         functools.partial(kernel, d),
         out_shape=(
             jax.ShapeDtypeStruct((ub, emb), F32),
             jax.ShapeDtypeStruct((ib, emb), F32),
-            jax.ShapeDtypeStruct((2, d.np, d.srows, d.scols), BF16),
+            jax.ShapeDtypeStruct((2, 2, d.np, d.srows, d.scols), BF16),
         ),
-        in_specs=[whole] * 7,
+        in_specs=[where, whole, whole, where, whole, where, where],
         out_specs=(whole,) * 3,
         scratch_shapes=scratch + sems,
         compiler_params=pltpu.CompilerParams(

time: 73.1 us -> 73 us (level)
  no operation moved by 1% of the time
where the time goes in v5:
time: 73 us; the launch traced here: 72.8 us
  Pallas kernels  72.2 us (99%)
    pallas_call x1, Pallas kernels, body(): pl.pallas_call(functools.partial(kernel, d), out_shape=(jax.ShapeDtypeStr...  69.8 us
    pallas_call x1, Pallas kernels, body(): pl.pallas_call(functools.partial(unpack, d), out_shape=(jax.ShapeDtypeStr...  2.36 us

profile of v5, /device:TPU:1, one launch (start us, length us, event | category | flops | bytes accessed | tf_op | source)
XLA Modules:
  0.0 72.8 jit_solution(1818833721309508542)
XLA Ops:
  0.6 69.8 %shard_map.102 = (f32[256,128]{1,0:T(8,128)}, f32[512,128]{1,0:T(8,128)}, bf16[2,2,16,16,256]{4,3,2,1,0:T(8,128)(2,1)}) custom-call(bf16[256,128]{1,0:T(8,128)(2,1)} %users_in.1, bf16[256]{0:T(256)(128)(2,1)} %weight_in.1, s32[256]{0:T(256)} %pos_in.1, bf16[512,128]{1,0:T(8,128)(2,1)} %feats_in.1, s32[512]{0:T(512)} %valid_in.1, bf16[128,1024]{1,0:T(8,128)(2,1)} %w_in_in.1, ...), custom_call_target="tpu_custom_call" | custom-call | flops 3221225472 | bytes 4194304 | tf_op jit(solution)/shard_map/pallas_call | solution.py:575
  70.5 2.4 %shard_map.103 = (f32[256,128]{1,0:T(8,128)}, f32[512,128]{1,0:T(8,128)}, f32[128,1024]{1,0:T(8,128)}, f32[1024,128]{1,0:T(8,128)}) custom-call(f32[256,128]{1,0:T(8,128)} %get-tuple-element.7.user_ref, f32[512,128]{1,0:T(8,128)} %get-tuple-element.8.item_ref, bf16[2,2,16,16,256]{4,3,2,1,0:T(8,128)(2,1)} %get-tuple-element.9.w_ref), custom_call_target="tpu_custom_call" | custom-call | tf_op jit(solution)/shard_map/pallas_call | solution.py:594

commit v6 on v5

--- a/solution.py
+++ b/solution.py
@@ -33,20 +33,21 @@
         self.items = self.nj * ib
         self.chunk = min(256, ib)
         self.nk = self.items // self.chunk
-        self.srows = max(16, emb // self.np)
-        self.scols = emb * (hid // 2) // self.np // self.srows
+        self.srows = 2 * emb // self.np
+        self.scols = hid // 2
+        self.groups = min(4, self.np)
 
 
 def kernel(
     d,
     users_in, weight_in, pos_in, feats_in, valid_in, w_in_in, w_out_in,
     out_user, out_item, out_w,
-    feats, w_in, w_out, users, meta, vecs, valid, bias, vec_t, hidden, slope, expo, grad,
+    feats, w_in, w_out, weight_v, pos_v, valid_v, item_v, users, meta, vecs, valid, bias, vec_t, hidden, slope, expo, grad,
     peak_s, total_s, factor, tile_s, weight_s,
     st_own, st_a, st_own2, st_b,
     gv_send, gv_recv, gv_own, gu_send, gu_recv, gu_sum, gu2_recv, gu_out,
     wg_own, wc_send, wc_recv, w1_send, w1_recv, wz, a1,
-    in_s, us_s, us_r, me_s, me_r, ve_s, ve_r, va_s, va_r, sa_s, sa_r, sb_s, sb_r,
+    in_s, out_s, us_s, us_r, me_s, me_r, ve_s, ve_r, va_s, va_r, sa_s, sa_r, sb_s, sb_r,
     gv_s, gv_r, gu_s, gu_r, g2_s, g2_r, g3_s, g3_r,
     wc_s, wc_r, w1_s, w1_r, wz_s, wz_r, w4_s, w4_r, w5_s, w5_r,
 ):
@@ -106,6 +107,15 @@
         each(n, lambda k: copy_in(k).wait_recv())
         flights[name][3] = True
 
+    def sent(*names):
+        for name in names:
+            if name in flights:
+                n, copy_out, _, landed = flights.pop(name)
+                each(n, lambda k: copy_out(k).wait_send())
+            else:
+                make, landed = singles.pop(name)
+                make().wait_send()
+
     tails = []
     singles = {}
 
@@ -120,16 +130,17 @@
     def finish():
         for wait in tails:
             wait()
-        for make, landed in singles.values():
-            if not landed:
-                make().wait_recv()
-            make().wait_send()
-        for name, (n, copy_out, _, landed) in flights.items():
-            if not landed:
+        for name in list(flights):
+            if not flights[name][3]:
                 land(name)
-            each(n, lambda k: copy_out(k).wait_send())
+            sent(name)
+        for name in list(singles):
+            if not singles[name][1]:
+                arrive(name)
+            sent(name)
 
     inputs = [(feats_in, feats), (w_in_in, w_in), (w_out_in, w_out), (users_in, users.at[z])]
+    inputs += [(weight_in, weight_v), (pos_in, pos_v), (valid_in, valid_v)]
     inputs = [pltpu.make_async_copy(src, dst, in_s.at[i]) for i, (src, dst) in enumerate(inputs)]
     for copy in inputs:
         copy.start()
@@ -143,11 +154,11 @@
     each(d.np, lambda k: greet(plane_dev(plane_peer(k))))
     greet(sibling)
 
-    pos = pos_in[...].reshape(1, ub)
-    meta[z] = jnp.concatenate([pos.astype(F32), weight_in[...].reshape(1, ub).astype(F32)], axis=0)
-    valid[0] = valid_in[...].reshape(1, ib).astype(F32)
     for copy in inputs:
         copy.wait()
+    pos = pos_v[...].reshape(1, ub)
+    meta[z] = jnp.concatenate([pos.astype(F32), weight_v[...].reshape(1, ub).astype(F32)], axis=0)
+    valid[0] = valid_v[...].reshape(1, ib).astype(F32)
     x = feats[...]
     pre = dot(x, w_in[...])
     hid_t = (pre * jax.nn.sigmoid(pre)).astype(BF16)
@@ -376,21 +387,35 @@
     lax.fori_loop(0, 4, grads, 0)
 
     us = ub // d.ng
+    zs = width // ub
+    turns = d.users // width
+    offsets = sorted(range(turns), key=lambda o: -min(o, turns - o))
 
     def gu_copy(k):
-        to = lax.rem(item + k, d.ng)
-        return remote(gu_send.at[to], gu_recv.at[k], gu_s.at[k], gu_r.at[k], dev(to, xl, z, core))
+        return remote(gu_send.at[z_peer(k)], gu_recv.at[k], gu_s.at[k], gu_r.at[k], z_dev(k))
 
     def user_terms(i, carry):
-        lanes = pl.ds(pl.multiple_of(i * width, width), width)
-        terms = dot(vec_t[...], grad[:, lanes]).T.astype(BF16)
-        for q in range(width // us):
-            at = q % d.ng
-            gu_send[at, i * (width // ub) + q // d.ng] = terms[q * us : (q + 1) * us, :]
+        offset = functools.reduce(lambda a, t: jnp.where(i == t, offsets[t], a), range(1, turns), offsets[0])
+        q = lax.rem(lax.div(z, zs) + offset, turns)
+        lanes = pl.ds(pl.multiple_of(q * width, width), width)
+        terms = dot(vec_t[...], grad[:, lanes]).T
+        for e in range(zs):
+            slot = q * zs + e
+            part = terms[e * ub : (e + 1) * ub, :]
+
+            @pl.when(slot == z)
+            def _():
+                gu_sum[...] = part
+
+            @pl.when(slot != z)
+            def _():
+                gu_send[slot] = part.astype(BF16)
+                gu_copy(back_by(slot, z, d.nz)).start()
+
         return carry
 
-    lax.fori_loop(0, d.users // width, user_terms, 0)
-    fly("gu", d.ng, gu_copy)
+    fly("gu", d.nz, gu_copy, start=False)
+    lax.fori_loop(0, turns, user_terms, 0)
 
     arrive("gv1")
     arrive("gv2")
@@ -415,108 +440,126 @@
     wc_send[0] = wg_own[0, :, other].astype(BF16)
     launch("wc0", functools.partial(wc_copy, 0))
 
-    sr, sc = d.srows, d.scols
-    cols = hc // sc
-
-    def w1_copy(m, k):
+    sr = d.srows
+    half = d.np // 2
+
+    def w1_copy(k):
         p = plane_peer(k)
-        return remote(w1_send.at[m, p], w1_recv.at[m, k], w1_s.at[m, k], w1_r.at[m, k], plane_dev(p))
+        return remote(w1_send.at[p], w1_recv.at[k], w1_s.at[k], w1_r.at[k], plane_dev(p))
 
     for m in (1, 0):
         arrive(f"wc{m}")
         total = (wg_own[m, :, mine] + wc_recv[m].astype(F32)).astype(BF16)
-        for c in range(cols):
-            rows = slice(c * d.np // cols, (c + 1) * d.np // cols)
-            w1_send[m, rows] = total[:, c * sc : (c + 1) * sc].reshape(d.np // cols, sr, sc)
-        fly(f"w1{m}", d.np, functools.partial(w1_copy, m))
-    out_item[...] = gv_own[...] + dot_t(hidden[...], w_in[...])
+        w1_send[m * half : (m + 1) * half] = total.reshape(half, sr, hc)
+    fly("w1", d.np, w1_copy)
+
+    def out_copy(i):
+        pairs = [(item_v, out_item), (gu_out, out_user), (a1.at[core], out_w.at[core]), (a1.at[1 - core], out_w.at[1 - core])]
+        return pltpu.make_async_copy(*pairs[i], out_s.at[i])
+
+    item_v[...] = gv_own[...] + dot_t(hidden[...], w_in[...])
+    out_copy(0).start()
+    tails.append(lambda: out_copy(0).wait())
+    tails.remove(users_sent)
+    users_sent()
+    sent("vecs1", "vecs2", "vecs3", "valid1", "valid2", "valid3", "st_a", "st_b")
+    sent("gv1", "gv2", "gv3", "wc0", "wc1")
+    land("w1")
+    part = w1_send[plane].astype(F32)
+    for k in range(1, d.np):
+        part = part + w1_recv[k].astype(F32)
+    wz[z] = part.astype(BF16)
+
+    def wz_copy(k, slot):
+        return remote(wz.at[slot], wz.at[slot], wz_s.at[k], wz_r.at[k], z_dev(k))
+
+    fly("wz", d.nz, lambda k: wz_copy(k, z), lambda k: wz_copy(k, back_by(z, k, d.nz)))
 
     land("gu")
-    gu_sum[...] = gu_send[item].astype(F32) + sum(gu_recv[k].astype(F32) for k in range(1, d.ng))
+    gu_sum[...] += sum(gu_recv[k].astype(F32) for k in range(1, d.nz))
+
+    def rows_of(i):
+        return pl.ds(pl.multiple_of(i * us, us), us)
 
     def g2_copy(k):
-        return remote(gu_sum.at[z_peer(k)], gu2_recv.at[k], g2_s.at[k], g2_r.at[k], z_dev(k))
-
-    fly("g2", d.nz, g2_copy)
-    def wz_copy(m, k, slot):
-        there = wz.at[m, slot]
-        return remote(there, there, wz_s.at[m, k], wz_r.at[m, k], z_dev(k))
-
+        to = lax.rem(item + k, d.ng)
+        return remote(gu_sum.at[rows_of(to), :], gu2_recv.at[k], g2_s.at[k], g2_r.at[k], group_dev(k))
+
+    fly("g2", d.ng, g2_copy)
+    sent("w1", "gu")
+    land("wz")
+    a1[core, plane] = sum(wz[k].astype(F32) for k in range(d.nz)).astype(BF16)
+
+    def w4_copy(k, slot):
+        there = a1.at[core, slot]
+        return remote(there, there, w4_s.at[k], w4_r.at[k], plane_dev(plane_peer(k)))
+
+    fly("w4", d.np, lambda k: w4_copy(k, plane), lambda k: w4_copy(k, back_by(plane, k, d.np)))
+
+    land("g2")
+    gu_out[rows_of(item), :] = gu_sum[rows_of(item), :] + sum(gu2_recv[k] for k in range(1, d.ng))
+
+    def g3_copy(k, at):
+        there = gu_out.at[rows_of(at), :]
+        return remote(there, there, g3_s.at[k], g3_r.at[k], group_dev(k))
+
+    fly("g3", d.ng, lambda k: g3_copy(k, item), lambda k: g3_copy(k, back_by(item, k, d.ng)))
+    sent("wz", "g2")
+
+    per_group = d.np // d.groups
+
+    def w5_copy(g, of):
+        there = a1.at[of, pl.ds(g * per_group, per_group)]
+        return remote(there, there, w5_s.at[g], w5_r.at[g], sibling)
+
+    for g in range(d.groups):
+        for slot in range(g * per_group, (g + 1) * per_group):
+
+            @pl.when(slot != plane)
+            def _():
+                w4_copy(back_by(plane, slot, d.np), slot).wait_recv()
+
+        w5_copy(g, core).start()
+    flights["w4"][3] = True
+    out_copy(2).start()
+    land("g3")
+    out_copy(1).start()
+    for g in range(d.groups):
+        w5_copy(g, 1 - core).wait_recv()
+    out_copy(3).start()
+
+    finish()
+    for g in range(d.groups):
+        w5_copy(g, core).wait_send()
+    for i in (1, 2, 3):
+        out_copy(i).wait()
+
+
+def unpack(d, user_ref, item_ref, w_ref, out_user, out_item, out_w_in, out_w_out, w_v, w_in_v, w_out_v, sems):
+    half, hc = d.np // 2, d.scols
+    copies = [pltpu.make_async_copy(w_ref.at[h, m], w_v.at[h, m], sems.at[2 * h + m]) for h in range(2) for m in range(2)]
+    copies += [
+        pltpu.make_async_copy(user_ref, out_user, sems.at[4]),
+        pltpu.make_async_copy(item_ref, out_item, sems.at[5]),
+    ]
+    for copy in copies:
+        copy.start()
+    results = [
+        pltpu.make_async_copy(w_in_v, out_w_in, sems.at[6]),
+        pltpu.make_async_copy(w_out_v, out_w_out, sems.at[7]),
+    ]
     for m in (1, 0):
-        land(f"w1{m}")
-        part = w1_send[m, plane].astype(F32)
-        for k in range(1, d.np):
-            part = part + w1_recv[m, k].astype(F32)
-        wz[m, z] = part.astype(BF16)
-        fly(
-            f"wz{m}",
-            d.nz,
-            lambda k, m=m: wz_copy(m, k, z),
-            lambda k, m=m: wz_copy(m, k, back_by(z, k, d.nz)),
-        )
-
-    land("g2")
-    mine = gu_sum[z]
-    for k in range(1, d.nz):
-        mine = mine + gu2_recv[k]
-    gu_out[item] = mine
-
-    def g3_copy(k, slot):
-        return remote(gu_out.at[slot], gu_out.at[slot], g3_s.at[k], g3_r.at[k], group_dev(k))
-
-    fly("g3", d.ng, lambda k: g3_copy(k, item), lambda k: g3_copy(k, back_by(item, k, d.ng)))
-
-    def w4_copy(m, k, slot):
-        there = a1.at[core, m, slot]
-        return remote(there, there, w4_s.at[m, k], w4_r.at[m, k], plane_dev(plane_peer(k)))
-
-    def w5_copy(m, k, slot, of):
-        there = a1.at[of, m, slot]
-        return remote(there, there, w5_s.at[m, k], w5_r.at[m, k], sibling)
-
-    for m in (1, 0):
-        land(f"wz{m}")
-        a1[core, m, plane] = sum(wz[m, k].astype(F32) for k in range(d.nz)).astype(BF16)
-        fly(
-            f"w4{m}",
-            d.np,
-            lambda k, m=m: w4_copy(m, k, plane),
-            lambda k, m=m: w4_copy(m, k, back_by(plane, k, d.np)),
-        )
-        w5_copy(m, 0, plane, core).start()
-
-    def hand_on(m, k):
-        slot = back_by(plane, k, d.np)
-        w4_copy(m, k, slot).wait_recv()
-        w5_copy(m, k, slot, core).start()
-
-    for m in (1, 0):
-        each(d.np, functools.partial(hand_on, m))
-        flights[f"w4{m}"][3] = True
-    land("g3")
-    out_user[...] = gu_out[...].reshape(ub, emb)
-    for m in (1, 0):
-        w5_copy(m, 0, plane, 1 - core).wait_recv()
-        each(d.np, lambda k: w5_copy(m, k, back_by(plane, k, d.np), 1 - core).wait_recv())
-    out_w[...] = a1[...]
-
-    finish()
-    for m in (1, 0):
-        w5_copy(m, 0, plane, core).wait_send()
-        each(d.np, lambda k: w5_copy(m, k, back_by(plane, k, d.np), core).wait_send())
-
-
-def unpack(d, user_ref, item_ref, w_ref, out_user, out_item, out_w_in, out_w_out):
-    out_user[...] = user_ref[...]
-    out_item[...] = item_ref[...]
-    hc, sc = d.hid // 2, d.scols
-    cols = hc // sc
-    for half in range(2):
-        for c in range(cols):
-            parts = slice(c * d.np // cols, (c + 1) * d.np // cols)
-            at = slice(half * hc + c * sc, half * hc + (c + 1) * sc)
-            out_w_in[:, at] = w_ref[half, 0, parts].astype(F32).reshape(d.emb, sc)
-            out_w_out[at, :] = w_ref[half, 1, parts].astype(F32).reshape(d.emb, sc).T
+        for h in range(2):
+            copies[2 * h + m].wait()
+            block = w_v[h, m].astype(F32).reshape(d.emb, hc)
+            at = slice(h * hc, (h + 1) * hc)
+            if m == 0:
+                w_in_v[:, at] = block
+            else:
+                w_out_v[at, :] = block.T
+        results[m].start()
+    for copy in copies[4:] + results:
+        copy.wait()
 
 
 def body(phys, user_vecs, row_weight, positive, item_feats, valid, w_in, w_out):
@@ -529,6 +572,10 @@
         vm((ib, emb), BF16),
         vm((emb, hid), BF16),
         vm((hid, emb), BF16),
+        vm((ub,), BF16),
+        vm((ub,), jnp.int32),
+        vm((ib,), jnp.int32),
+        vm((ib, emb), F32),
         vm((d.nz, ub, emb), BF16),
         vm((d.nz, 2, ub), F32),
         vm((d.nj, ib, emb), BF16),
@@ -551,36 +598,33 @@
         vm((d.nj, ib, emb), BF16),
         vm((d.nj, ib, emb), BF16),
         vm((ib, emb), F32),
-        vm((d.ng, d.nz, us, emb), BF16),
-        vm((d.ng, d.nz, us, emb), BF16),
-        vm((d.nz, us, emb), F32),
-        vm((d.nz, us, emb), F32),
+        vm((d.nz, ub, emb), BF16),
+        vm((d.nz, ub, emb), BF16),
+        vm((ub, emb), F32),
         vm((d.ng, us, emb), F32),
+        vm((ub, emb), F32),
         vm((2, emb, hid), F32),
         vm((2, emb, hid // 2), BF16),
         vm((2, emb, hid // 2), BF16),
+        vm((d.np, d.srows, d.scols), BF16),
+        vm((d.np, d.srows, d.scols), BF16),
+        vm((d.nz, d.srows, d.scols), BF16),
         vm((2, d.np, d.srows, d.scols), BF16),
-        vm((2, d.np, d.srows, d.scols), BF16),
-        vm((2, d.nz, d.srows, d.scols), BF16),
-        vm((2, 2, d.np, d.srows, d.scols), BF16),
     ]
     dma = pltpu.SemaphoreType.DMA
-    sems = [dma((4,))]
-    for n in (d.nz, d.nz, d.nj, d.nj, d.ng, d.nz, d.nj, d.ng, d.nz, d.ng, 2):
+    sems = [dma((7,)), dma((4,))]
+    for n in (d.nz, d.nz, d.nj, d.nj, d.ng, d.nz, d.nj, d.nz, d.ng, d.ng, 2, d.np, d.nz, d.np, d.groups):
         sems += [dma((n,)), dma((n,))]
-    for n in (d.np, d.nz, d.np, d.np):
-        sems += [dma((2, n)), dma((2, n))]
-    whole = pl.BlockSpec(memory_space=pltpu.VMEM)
     where = pl.BlockSpec(memory_space=pl.ANY)
     parts = pl.pallas_call(
         functools.partial(kernel, d),
         out_shape=(
             jax.ShapeDtypeStruct((ub, emb), F32),
             jax.ShapeDtypeStruct((ib, emb), F32),
-            jax.ShapeDtypeStruct((2, 2, d.np, d.srows, d.scols), BF16),
+            jax.ShapeDtypeStruct((2, d.np, d.srows, d.scols), BF16),
         ),
-        in_specs=[where, whole, whole, where, whole, where, where],
-        out_specs=(whole,) * 3,
+        in_specs=[where] * 7,
+        out_specs=(where,) * 3,
         scratch_shapes=scratch + sems,
         compiler_params=pltpu.CompilerParams(
             collective_id=0, has_side_effects=True, vmem_limit_bytes=56 * 1024 * 1024
@@ -591,6 +635,8 @@
             transcendentals=d.users * d.items,
         ),
     )(user_vecs, row_weight, positive, item_feats, valid, w_in, w_out)
+    user, item, weights = parts
+    weights = weights.reshape(2, 2, d.np // 2, d.srows, d.scols)
     return pl.pallas_call(
         functools.partial(unpack, d),
         out_shape=(
@@ -599,9 +645,15 @@
             jax.ShapeDtypeStruct((emb, hid), F32),
             jax.ShapeDtypeStruct((hid, emb), F32),
         ),
-        in_specs=[whole] * 3,
-        out_specs=(whole,) * 4,
-    )(*parts)
+        in_specs=[where] * 3,
+        out_specs=(where,) * 4,
+        scratch_shapes=[
+            vm(weights.shape, BF16),
+            vm((emb, hid), F32),
+            vm((hid, emb), F32),
+            dma((8,)),
+        ],
+    )(user, item, weights)
 
 
 def build(mesh, phys):

time: 73 us -> 80.9 us (1.11)
  Pallas kernels: 72.2 us -> 80.2 us
    pallas_call x1, Pallas kernels: 2.36 us -> 13.1 us  [body(): pl.pallas_call(functools.partial(unpack, d), out_shape=(jax.ShapeDtypeStr...]
    pallas_call x1, Pallas kernels: 69.8 us -> 67.1 us  [body(): pl.pallas_call(functools.partial(kernel, d), out_shape=(jax.ShapeDtypeStr...]
where the time goes in v6:
time: 80.9 us; the launch traced here: 80.8 us
  Pallas kernels  80.2 us (99%)
    pallas_call x1, Pallas kernels, body(): pl.pallas_call(functools.partial(kernel, d), out_shape=(jax.ShapeDtypeStr...  67.1 us
    pallas_call x1, Pallas kernels, body(): pl.pallas_call(functools.partial(unpack, d), out_shape=(jax.ShapeDtypeStr...  13.1 us

profile of v6, /device:TPU:1, one launch (start us, length us, event | category | flops | bytes accessed | tf_op | source)
XLA Modules:
  0.0 80.8 jit_solution(5249011391607997770)
XLA Ops:
  0.6 67.1 %shard_map.102 = (f32[256,128]{1,0:T(8,128)}, f32[512,128]{1,0:T(8,128)}, bf16[2,16,16,512]{3,2,1,0:T(8,128)(2,1)}) custom-call(bf16[256,128]{1,0:T(8,128)(2,1)} %users_in.1, bf16[256]{0:T(256)(128)(2,1)} %weight_in.1, s32[256]{0:T(256)} %pos_in.1, bf16[512,128]{1,0:T(8,128)(2,1)} %feats_in.1, s32[512]{0:T(512)} %valid_in.1, bf16[128,1024]{1,0:T(8,128)(2,1)} %w_in_in.1, ...), custom_call_target="tpu_custom_call" | custom-call | flops 3221225472 | bytes 4194304 | tf_op jit(solution)/shard_map/pallas_call | solution.py:619
  67.7 13.1 %shard_map.103 = (f32[256,128]{1,0:T(8,128)}, f32[512,128]{1,0:T(8,128)}, f32[128,1024]{1,0:T(8,128)}, f32[1024,128]{1,0:T(8,128)}) custom-call(f32[256,128]{1,0:T(8,128)} %get-tuple-element.7.user_ref, f32[512,128]{1,0:T(8,128)} %get-tuple-element.8.item_ref, bf16[2,2,8,16,512]{4,3,2,1,0:T(8,128)(2,1)} %bitcast.1), custom_call_target="tpu_custom_call" | custom-call | tf_op jit(solution)/shard_map/pallas_call | solution.py:640

commit v7 on v6

--- a/solution.py
+++ b/solution.py
@@ -535,30 +535,29 @@
         out_copy(i).wait()
 
 
-def unpack(d, user_ref, item_ref, w_ref, out_user, out_item, out_w_in, out_w_out, w_v, w_in_v, w_out_v, sems):
+def unpack(d, user_ref, item_ref, w_ref, out_user, out_item, out_w_in, out_w_out, user_v, item_v, w_v, w_in_v, w_out_v, sems):
     half, hc = d.np // 2, d.scols
-    copies = [pltpu.make_async_copy(w_ref.at[h, m], w_v.at[h, m], sems.at[2 * h + m]) for h in range(2) for m in range(2)]
-    copies += [
-        pltpu.make_async_copy(user_ref, out_user, sems.at[4]),
-        pltpu.make_async_copy(item_ref, out_item, sems.at[5]),
-    ]
-    for copy in copies:
+    loads = [(w_ref.at[h, m], w_v.at[h, m]) for m in (1, 0) for h in range(2)]
+    loads += [(item_ref, item_v), (user_ref, user_v)]
+    loads = [pltpu.make_async_copy(src, dst, sems.at[i]) for i, (src, dst) in enumerate(loads)]
+    for copy in loads:
         copy.start()
-    results = [
-        pltpu.make_async_copy(w_in_v, out_w_in, sems.at[6]),
-        pltpu.make_async_copy(w_out_v, out_w_out, sems.at[7]),
-    ]
+    stores = [(w_out_v, out_w_out), (w_in_v, out_w_in), (item_v, out_item), (user_v, out_user)]
+    stores = [pltpu.make_async_copy(src, dst, sems.at[6 + i]) for i, (src, dst) in enumerate(stores)]
     for m in (1, 0):
         for h in range(2):
-            copies[2 * h + m].wait()
+            loads[2 * (1 - m) + h].wait()
             block = w_v[h, m].astype(F32).reshape(d.emb, hc)
             at = slice(h * hc, (h + 1) * hc)
             if m == 0:
                 w_in_v[:, at] = block
             else:
                 w_out_v[at, :] = block.T
-        results[m].start()
-    for copy in copies[4:] + results:
+        stores[1 - m].start()
+    for i in (4, 5):
+        loads[i].wait()
+        stores[i - 2].start()
+    for copy in stores:
         copy.wait()
 
 
@@ -648,10 +647,12 @@
         in_specs=[where] * 3,
         out_specs=(where,) * 4,
         scratch_shapes=[
+            vm((ub, emb), F32),
+            vm((ib, emb), F32),
             vm(weights.shape, BF16),
             vm((emb, hid), F32),
             vm((hid, emb), F32),
-            dma((8,)),
+            dma((10,)),
         ],
     )(user, item, weights)
 

time: 80.9 us -> 70.1 us (0.87)
  Pallas kernels: 80.2 us -> 69.4 us
    pallas_call x1, Pallas kernels: 13.1 us -> 2.29 us  [body(): pl.pallas_call(functools.partial(unpack, d), out_shape=(jax.ShapeDtypeStr...]
where the time goes in v7:
time: 70.1 us; the launch traced here: 70 us
  Pallas kernels  69.4 us (99%)
    pallas_call x1, Pallas kernels, body(): pl.pallas_call(functools.partial(kernel, d), out_shape=(jax.ShapeDtypeStr...  67.1 us
    pallas_call x1, Pallas kernels, body(): pl.pallas_call(functools.partial(unpack, d), out_shape=(jax.ShapeDtypeStr...  2.29 us

profile of v7, /device:TPU:1, one launch (start us, length us, event | category | flops | bytes accessed | tf_op | source)
XLA Modules:
  0.0 70.0 jit_solution(4308654937688843856)
XLA Ops:
  0.6 67.1 %shard_map.102 = (f32[256,128]{1,0:T(8,128)}, f32[512,128]{1,0:T(8,128)}, bf16[2,16,16,512]{3,2,1,0:T(8,128)(2,1)}) custom-call(bf16[256,128]{1,0:T(8,128)(2,1)} %users_in.1, bf16[256]{0:T(256)(128)(2,1)} %weight_in.1, s32[256]{0:T(256)} %pos_in.1, bf16[512,128]{1,0:T(8,128)(2,1)} %feats_in.1, s32[512]{0:T(512)} %valid_in.1, bf16[128,1024]{1,0:T(8,128)(2,1)} %w_in_in.1, ...), custom_call_target="tpu_custom_call" | custom-call | flops 3221225472 | bytes 4194304 | tf_op jit(solution)/shard_map/pallas_call | solution.py:618
  67.7 2.3 %shard_map.103 = (f32[256,128]{1,0:T(8,128)}, f32[512,128]{1,0:T(8,128)}, f32[128,1024]{1,0:T(8,128)}, f32[1024,128]{1,0:T(8,128)}) custom-call(f32[256,128]{1,0:T(8,128)} %get-tuple-element.7.user_ref, f32[512,128]{1,0:T(8,128)} %get-tuple-element.8.item_ref, bf16[2,2,8,16,512]{4,3,2,1,0:T(8,128)(2,1)} %bitcast.1), custom_call_target="tpu_custom_call" | custom-call | tf_op jit(solution)/shard_map/pallas_call | solution.py:639

commit v8 on v7

--- a/solution.py
+++ b/solution.py
@@ -36,6 +36,7 @@
         self.srows = 2 * emb // self.np
         self.scols = hid // 2
         self.groups = min(4, self.np)
+        self.nfar = max(0, self.nz - 5)
 
 
 def kernel(
@@ -45,11 +46,11 @@
     feats, w_in, w_out, weight_v, pos_v, valid_v, item_v, users, meta, vecs, valid, bias, vec_t, hidden, slope, expo, grad,
     peak_s, total_s, factor, tile_s, weight_s,
     st_own, st_a, st_own2, st_b,
-    gv_send, gv_recv, gv_own, gu_send, gu_recv, gu_sum, gu2_recv, gu_out,
-    wg_own, wc_send, wc_recv, w1_send, w1_recv, wz, a1,
+    gv_send, gv_recv, gv_own, gu_send, gu_recv, gu_sum, gu2_recv, gu_out, gf_send, gf_recv, gf_sum, gf2_recv,
+    wg_own, pre_s, feats_t, wc_send, wc_recv, w1_send, w1_recv, wz, a1,
     in_s, out_s, us_s, us_r, me_s, me_r, ve_s, ve_r, va_s, va_r, sa_s, sa_r, sb_s, sb_r,
     gv_s, gv_r, gu_s, gu_r, g2_s, g2_r, g3_s, g3_r,
-    wc_s, wc_r, w1_s, w1_r, wz_s, wz_r, w4_s, w4_r, w5_s, w5_r,
+    wc_s, wc_r, w1_s, w1_r, wz_s, wz_r, w4_s, w4_r, w5_s, w5_r, gf_s, gf_r, f2_s, f2_r,
 ):
     ub, ib, emb, hid = d.ub, d.ib, d.emb, d.hid
     item = lax.axis_index("item")
@@ -82,6 +83,7 @@
 
     sibling = dev(item, xl, z, 1 - core)
     across = dev(item, 1 - xl, z, core)
+    diagonal = dev(item, 1 - xl, z, 1 - core)
 
     def remote(src, dst, send, recv, to):
         return pltpu.make_async_remote_copy(
@@ -139,20 +141,21 @@
                 arrive(name)
             sent(name)
 
+    barrier = pltpu.get_barrier_semaphore()
+
+    def greet(to):
+        pl.semaphore_signal(barrier, inc=1, device_id=to, device_id_type=MESH)
+
+    each(d.nz, lambda k: greet(z_dev(k)))
+    each(d.np, lambda k: greet(plane_dev(plane_peer(k))))
+    greet(sibling)
+    greet(diagonal)
+
     inputs = [(feats_in, feats), (w_in_in, w_in), (w_out_in, w_out), (users_in, users.at[z])]
     inputs += [(weight_in, weight_v), (pos_in, pos_v), (valid_in, valid_v)]
     inputs = [pltpu.make_async_copy(src, dst, in_s.at[i]) for i, (src, dst) in enumerate(inputs)]
     for copy in inputs:
         copy.start()
-
-    barrier = pltpu.get_barrier_semaphore()
-
-    def greet(to):
-        pl.semaphore_signal(barrier, inc=1, device_id=to, device_id_type=MESH)
-
-    each(d.nz, lambda k: greet(z_dev(k)))
-    each(d.np, lambda k: greet(plane_dev(plane_peer(k))))
-    greet(sibling)
 
     for copy in inputs:
         copy.wait()
@@ -165,7 +168,7 @@
     hidden[...] = hid_t
     slope[...] = pre
     vecs[0] = (x.astype(F32) + dot(hid_t, w_out[...])).astype(BF16)
-    pl.semaphore_wait(barrier, d.nz - 1 + d.np - 1 + 1)
+    pl.semaphore_wait(barrier, d.nz - 1 + d.np - 1 + 2)
 
     far = d.nz // 2
     direct = [k for k in (2, d.nz - 2, 1, d.nz - 1) if 0 < k < d.nz]
@@ -340,6 +343,7 @@
     pre = slope[...]
     sigma = jax.nn.sigmoid(pre)
     slope[...] = sigma * (1.0 + pre * (1.0 - sigma))
+    feats_t[...] = feats[...].astype(F32).T.astype(BF16)
     land("st_a")
     st_own2[...] = merge([st_own[...]] + [st_a[k] for k in range(1, d.ng)])
     fly("st_b", d.nz, st_b_copy)
@@ -348,8 +352,21 @@
     for c in range(d.nk):
         factor[c] = weight_s[...] * jnp.exp(peak_s[c] - log_total)
 
-    def gv_copy(j):
-        return remote(gv_send.at[j], gv_recv.at[j], gv_s.at[j], gv_r.at[j], across if j == 2 else sibling)
+    lone = ib // 4
+
+    def gv_copy(name):
+        i, rows, slot, to = {
+            "gv3": (3, slice(lone, ib), 3, sibling),
+            "gv3_lone": (3, slice(0, lone), 0, diagonal),
+            "gv2": (2, slice(lone, ib), 2, across),
+            "gv2_lone": (2, slice(0, lone), 2, across),
+            "gv1": (1, slice(0, ib), 1, sibling),
+        }[name]
+        n = ("gv1", "gv2", "gv3", "gv2_lone", "gv3_lone").index(name)
+        return remote(gv_send.at[i, rows], gv_recv.at[slot, rows], gv_s.at[n], gv_r.at[n], to)
+
+    def gv_launch(name):
+        launch(name, functools.partial(gv_copy, name))
 
     width = min(512, d.users)
     per = ib // d.chunk
@@ -369,24 +386,31 @@
             acc = acc + dot(g, users[...].reshape(d.users, emb)[lanes, :])
         gv_own[...] = acc
 
-        for at, i in ((0, 3), (2, 1)):
-
-            @pl.when(t == at)
-            def _():
-                gv_send[i] = gv_own[...].astype(BF16)
-                launch(f"gv{i}", functools.partial(gv_copy, i))
+        @pl.when(t == 0)
+        def _():
+            gv_send[3] = gv_own[...].astype(BF16)
+            gv_launch("gv3_lone")
+            gv_launch("gv3")
 
         @pl.when(t == 1)
         def _():
+            gv_send[2, :lone] = gv_own[:lone, :].astype(BF16)
+            gv_launch("gv2_lone")
             arrive("gv3")
-            gv_send[2] = (gv_own[...] + gv_recv[3].astype(F32)).astype(BF16)
-            launch("gv2", functools.partial(gv_copy, 2))
+            gv_send[2, lone:] = (gv_own[lone:, :] + gv_recv[3, lone:, :].astype(F32)).astype(BF16)
+            gv_launch("gv2")
+
+        @pl.when(t == 2)
+        def _():
+            gv_send[1] = gv_own[...].astype(BF16)
+            gv_launch("gv1")
 
         return carry
 
     lax.fori_loop(0, 4, grads, 0)
 
     us = ub // d.ng
+    nfar = d.nfar
     zs = width // ub
     turns = d.users // width
     offsets = sorted(range(turns), key=lambda o: -min(o, turns - o))
@@ -407,22 +431,45 @@
             def _():
                 gu_sum[...] = part
 
-            @pl.when(slot != z)
+            k = back_by(slot, z, d.nz)
+            is_near = (slot != z) & ((k < 3) | (k > d.nz - 3))
+
+            @pl.when(is_near)
             def _():
                 gu_send[slot] = part.astype(BF16)
-                gu_copy(back_by(slot, z, d.nz)).start()
+                gu_copy(k).start()
+
+            if nfar:
+
+                @pl.when((k >= 3) & (k <= d.nz - 3))
+                def _():
+                    for g in range(d.ng):
+                        gf_send[g, k - 3] = part[g * us : (g + 1) * us, :].astype(BF16)
 
         return carry
 
-    fly("gu", d.nz, gu_copy, start=False)
+    def near_hops(i):
+        return jnp.where(i < 3, i, i + nfar)
+
+    def gf_copy(k):
+        to = lax.rem(item + k, d.ng)
+        return remote(gf_send.at[to], gf_recv.at[k], gf_s.at[k], gf_r.at[k], dev(to, xl, z, core))
+
+    def gf2_copy(i):
+        return remote(gf_sum.at[i - 1], gf2_recv.at[i - 1], f2_s.at[i], f2_r.at[i], z_dev(i + 2))
+
+    fly("gu", d.nz - nfar, lambda i: gu_copy(near_hops(i)), start=False)
     lax.fori_loop(0, turns, user_terms, 0)
-
-    arrive("gv1")
-    arrive("gv2")
+    if nfar:
+        fly("gf", d.ng, gf_copy)
+
+    for name in ("gv1", "gv3_lone", "gv2_lone", "gv2"):
+        arrive(name)
     gv = gv_own[...] + gv_recv[1].astype(F32) + gv_recv[2].astype(F32)
-    gv = gv.astype(BF16)
+    gv_own[...] = gv
+    gv_own[:lone, :] += gv_recv[0, :lone, :].astype(F32)
+    gv = gv_own[...].astype(BF16)
     gv_own[...] = gv.astype(F32)
-    gv_t = gv_own[...].T.astype(BF16)
     hc = hid // 2
     mine = pl.ds(pl.multiple_of(core * hc, hc), hc)
     other = pl.ds(pl.multiple_of((1 - core) * hc, hc), hc)
@@ -430,15 +477,14 @@
     def wc_copy(m):
         return remote(wc_send.at[m], wc_recv.at[m], wc_s.at[m], wc_r.at[m], sibling)
 
-    wg_own[1] = dot(gv_t, hidden[...])
-    wc_send[1] = wg_own[1, :, other].astype(BF16)
+    pre_s[...] = (dot_t(gv, w_out[...]) * slope[...]).astype(BF16)
+    wc_send[0] = dot(feats_t[...], pre_s[:, other]).astype(BF16)
+    launch("wc0", functools.partial(wc_copy, 0))
+    gv_t = gv_own[...].T.astype(BF16)
+    wc_send[1] = dot(gv_t, hidden[:, other]).astype(BF16)
     launch("wc1", functools.partial(wc_copy, 1))
-
-    pre = (dot_t(gv, w_out[...]) * slope[...]).astype(BF16)
-    hidden[...] = pre
-    wg_own[0] = dot(feats[...].astype(F32).T.astype(BF16), pre)
-    wc_send[0] = wg_own[0, :, other].astype(BF16)
-    launch("wc0", functools.partial(wc_copy, 0))
+    wg_own[0] = dot(feats_t[...], pre_s[:, mine])
+    wg_own[1] = dot(gv_t, hidden[:, mine])
 
     sr = d.srows
     half = d.np // 2
@@ -447,23 +493,36 @@
         p = plane_peer(k)
         return remote(w1_send.at[p], w1_recv.at[k], w1_s.at[k], w1_r.at[k], plane_dev(p))
 
-    for m in (1, 0):
+    fly("w1", d.np, w1_copy, start=False)
+    for m in (0, 1):
         arrive(f"wc{m}")
-        total = (wg_own[m, :, mine] + wc_recv[m].astype(F32)).astype(BF16)
+        total = (wg_own[m] + wc_recv[m].astype(F32)).astype(BF16)
         w1_send[m * half : (m + 1) * half] = total.reshape(half, sr, hc)
-    fly("w1", d.np, w1_copy)
+
+        def start(k):
+            p = plane_peer(k)
+
+            @pl.when(p < half if m == 0 else p >= half)
+            def _():
+                w1_copy(k).start()
+
+        each(d.np, start)
 
     def out_copy(i):
         pairs = [(item_v, out_item), (gu_out, out_user), (a1.at[core], out_w.at[core]), (a1.at[1 - core], out_w.at[1 - core])]
         return pltpu.make_async_copy(*pairs[i], out_s.at[i])
 
-    item_v[...] = gv_own[...] + dot_t(hidden[...], w_in[...])
+    item_v[...] = gv_own[...] + dot_t(pre_s[...], w_in[...])
     out_copy(0).start()
     tails.append(lambda: out_copy(0).wait())
     tails.remove(users_sent)
     users_sent()
     sent("vecs1", "vecs2", "vecs3", "valid1", "valid2", "valid3", "st_a", "st_b")
-    sent("gv1", "gv2", "gv3", "wc0", "wc1")
+    sent("gv1", "gv2", "gv3", "gv2_lone", "gv3_lone", "wc0", "wc1")
+    if nfar:
+        land("gf")
+        gf_sum[...] = gf_send[item].astype(F32) + sum(gf_recv[k].astype(F32) for k in range(1, d.ng))
+        fly("gf2", nfar + 1, gf2_copy)
     land("w1")
     part = w1_send[plane].astype(F32)
     for k in range(1, d.np):
@@ -476,7 +535,7 @@
     fly("wz", d.nz, lambda k: wz_copy(k, z), lambda k: wz_copy(k, back_by(z, k, d.nz)))
 
     land("gu")
-    gu_sum[...] += sum(gu_recv[k].astype(F32) for k in range(1, d.nz))
+    gu_sum[...] += sum(gu_recv[k].astype(F32) for k in range(1, d.nz) if k < 3 or k > d.nz - 3)
 
     def rows_of(i):
         return pl.ds(pl.multiple_of(i * us, us), us)
@@ -497,7 +556,12 @@
     fly("w4", d.np, lambda k: w4_copy(k, plane), lambda k: w4_copy(k, back_by(plane, k, d.np)))
 
     land("g2")
-    gu_out[rows_of(item), :] = gu_sum[rows_of(item), :] + sum(gu2_recv[k] for k in range(1, d.ng))
+    total = gu_sum[rows_of(item), :] + sum(gu2_recv[k] for k in range(1, d.ng))
+    if nfar:
+        land("gf2")
+        total = total + sum(gf2_recv[i] for i in range(nfar))
+        sent("gf", "gf2")
+    gu_out[rows_of(item), :] = total
 
     def g3_copy(k, at):
         there = gu_out.at[rows_of(at), :]
@@ -602,7 +666,13 @@
         vm((ub, emb), F32),
         vm((d.ng, us, emb), F32),
         vm((ub, emb), F32),
-        vm((2, emb, hid), F32),
+        vm((d.ng, max(1, d.nfar), us, emb), BF16),
+        vm((d.ng, max(1, d.nfar), us, emb), BF16),
+        vm((max(1, d.nfar), us, emb), F32),
+        vm((max(1, d.nfar), us, emb), F32),
+        vm((2, emb, hid // 2), F32),
+        vm((ib, hid), BF16),
+        vm((emb, ib), BF16),
         vm((2, emb, hid // 2), BF16),
         vm((2, emb, hid // 2), BF16),
         vm((d.np, d.srows, d.scols), BF16),
@@ -612,7 +682,7 @@
     ]
     dma = pltpu.SemaphoreType.DMA
     sems = [dma((7,)), dma((4,))]
-    for n in (d.nz, d.nz, d.nj, d.nj, d.ng, d.nz, d.nj, d.nz, d.ng, d.ng, 2, d.np, d.nz, d.np, d.groups):
+    for n in (d.nz, d.nz, d.nj, d.nj, d.ng, d.nz, 5, d.nz, d.ng, d.ng, 2, d.np, d.nz, d.np, d.groups, d.ng, d.nz):
         sems += [dma((n,)), dma((n,))]
     where = pl.BlockSpec(memory_space=pl.ANY)
     parts = pl.pallas_call(

time: 70.1 us -> 68.6 us (0.979)
  Pallas kernels: 69.4 us -> 67.8 us
    pallas_call x1, Pallas kernels: 67.1 us -> 65.5 us  [body(): pl.pallas_call(functools.partial(kernel, d), out_shape=(jax.ShapeDtypeStr...]
where the time goes in v8:
time: 68.6 us; the launch traced here: 68.5 us
  Pallas kernels  67.8 us (99%)
    pallas_call x1, Pallas kernels, body(): pl.pallas_call(functools.partial(kernel, d), out_shape=(jax.ShapeDtypeStr...  65.5 us
    pallas_call x1, Pallas kernels, body(): pl.pallas_call(functools.partial(unpack, d), out_shape=(jax.ShapeDtypeStr...  2.29 us

profile of v8, /device:TPU:1, one launch (start us, length us, event | category | flops | bytes accessed | tf_op | source)
XLA Modules:
  0.0 68.5 jit_solution(11317225624014448170)
XLA Ops:
  0.6 65.5 %shard_map.102 = (f32[256,128]{1,0:T(8,128)}, f32[512,128]{1,0:T(8,128)}, bf16[2,16,16,512]{3,2,1,0:T(8,128)(2,1)}) custom-call(bf16[256,128]{1,0:T(8,128)(2,1)} %users_in.1, bf16[256]{0:T(256)(128)(2,1)} %weight_in.1, s32[256]{0:T(256)} %pos_in.1, bf16[512,128]{1,0:T(8,128)(2,1)} %feats_in.1, s32[512]{0:T(512)} %valid_in.1, bf16[128,1024]{1,0:T(8,128)(2,1)} %w_in_in.1, ...), custom_call_target="tpu_custom_call" | custom-call | flops 3221225472 | bytes 4194304 | tf_op jit(solution)/shard_map/pallas_call | solution.py:688
  66.2 2.3 %shard_map.103 = (f32[256,128]{1,0:T(8,128)}, f32[512,128]{1,0:T(8,128)}, f32[128,1024]{1,0:T(8,128)}, f32[1024,128]{1,0:T(8,128)}) custom-call(f32[256,128]{1,0:T(8,128)} %get-tuple-element.7.user_ref, f32[512,128]{1,0:T(8,128)} %get-tuple-element.8.item_ref, bf16[2,2,8,16,512]{4,3,2,1,0:T(8,128)(2,1)} %bitcast.1), custom_call_target="tpu_custom_call" | custom-call | tf_op jit(solution)/shard_map/pallas_call | solution.py:709

commit v9 on v8

--- a/solution.py
+++ b/solution.py
@@ -287,6 +287,12 @@
                         hand_on_users(k)
                     enter(slot)
 
+        @pl.when(i == ng - 1)
+        def _():
+            vec_arrives(2)
+            launch("vecs3", functools.partial(vecs_copy, 3))
+            launch("valid3", functools.partial(valid_copy, 3))
+
         for q in range(len(groups[0])):
             k = functools.reduce(lambda a, g: jnp.where(turn == g, groups[g][q], a), range(1, ng), groups[0][q])
             slot = back_by(z, k, d.nz)
@@ -310,9 +316,6 @@
     set_bias(1)
     score(1, z)
     lax.fori_loop(0, ng, early_steps, 0)
-    vec_arrives(2)
-    launch("vecs3", functools.partial(vecs_copy, 3))
-    launch("valid3", functools.partial(valid_copy, 3))
     set_bias(2)
     score(2, z)
     vec_arrives(3)

time: 68.6 us -> 68.9 us (level)
  no operation moved by 1% of the time
where the time goes in v9:
time: 68.9 us; the launch traced here: 68.8 us
  Pallas kernels  68.2 us (99%)
    pallas_call x1, Pallas kernels, body(): pl.pallas_call(functools.partial(kernel, d), out_shape=(jax.ShapeDtypeStr...  65.9 us
    pallas_call x1, Pallas kernels, body(): pl.pallas_call(functools.partial(unpack, d), out_shape=(jax.ShapeDtypeStr...  2.29 us

profile of v9, /device:TPU:1, one launch (start us, length us, event | category | flops | bytes accessed | tf_op | source)
XLA Modules:
  0.0 68.8 jit_solution(12197114678170866194)
XLA Ops:
  0.6 65.9 %shard_map.102 = (f32[256,128]{1,0:T(8,128)}, f32[512,128]{1,0:T(8,128)}, bf16[2,16,16,512]{3,2,1,0:T(8,128)(2,1)}) custom-call(bf16[256,128]{1,0:T(8,128)(2,1)} %users_in.1, bf16[256]{0:T(256)(128)(2,1)} %weight_in.1, s32[256]{0:T(256)} %pos_in.1, bf16[512,128]{1,0:T(8,128)(2,1)} %feats_in.1, s32[512]{0:T(512)} %valid_in.1, bf16[128,1024]{1,0:T(8,128)(2,1)} %w_in_in.1, ...), custom_call_target="tpu_custom_call" | custom-call | flops 3221225472 | bytes 4194304 | tf_op jit(solution)/shard_map/pallas_call | solution.py:691
  66.5 2.3 %shard_map.103 = (f32[256,128]{1,0:T(8,128)}, f32[512,128]{1,0:T(8,128)}, f32[128,1024]{1,0:T(8,128)}, f32[1024,128]{1,0:T(8,128)}) custom-call(f32[256,128]{1,0:T(8,128)} %get-tuple-element.7.user_ref, f32[512,128]{1,0:T(8,128)} %get-tuple-element.8.item_ref, bf16[2,2,8,16,512]{4,3,2,1,0:T(8,128)(2,1)} %bitcast.1), custom_call_target="tpu_custom_call" | custom-call | tf_op jit(solution)/shard_map/pallas_call | solution.py:712

commit v10 on v9

--- a/solution.py
+++ b/solution.py
@@ -512,7 +512,7 @@
         each(d.np, start)
 
     def out_copy(i):
-        pairs = [(item_v, out_item), (gu_out, out_user), (a1.at[core], out_w.at[core]), (a1.at[1 - core], out_w.at[1 - core])]
+        pairs = [(item_v, out_item), (gu_out, out_user), (a1, out_w.at[core])]
         return pltpu.make_async_copy(*pairs[i], out_s.at[i])
 
     item_v[...] = gv_own[...] + dot_t(pre_s[...], w_in[...])
@@ -550,10 +550,10 @@
     fly("g2", d.ng, g2_copy)
     sent("w1", "gu")
     land("wz")
-    a1[core, plane] = sum(wz[k].astype(F32) for k in range(d.nz)).astype(BF16)
+    a1[plane] = sum(wz[k].astype(F32) for k in range(d.nz)).astype(BF16)
 
     def w4_copy(k, slot):
-        there = a1.at[core, slot]
+        there = a1.at[slot]
         return remote(there, there, w4_s.at[k], w4_r.at[k], plane_dev(plane_peer(k)))
 
     fly("w4", d.np, lambda k: w4_copy(k, plane), lambda k: w4_copy(k, back_by(plane, k, d.np)))
@@ -576,8 +576,8 @@
     per_group = d.np // d.groups
 
     def w5_copy(g, of):
-        there = a1.at[of, pl.ds(g * per_group, per_group)]
-        return remote(there, there, w5_s.at[g], w5_r.at[g], sibling)
+        slots = pl.ds(g * per_group, per_group)
+        return remote(a1.at[slots], out_w.at[of, slots], w5_s.at[g], w5_r.at[g], sibling)
 
     for g in range(d.groups):
         for slot in range(g * per_group, (g + 1) * per_group):
@@ -593,12 +593,11 @@
     out_copy(1).start()
     for g in range(d.groups):
         w5_copy(g, 1 - core).wait_recv()
-    out_copy(3).start()
 
     finish()
     for g in range(d.groups):
         w5_copy(g, core).wait_send()
-    for i in (1, 2, 3):
+    for i in (1, 2):
         out_copy(i).wait()
 
 
@@ -681,7 +680,7 @@
         vm((d.np, d.srows, d.scols), BF16),
         vm((d.np, d.srows, d.scols), BF16),
         vm((d.nz, d.srows, d.scols), BF16),
-        vm((2, d.np, d.srows, d.scols), BF16),
+        vm((d.np, d.srows, d.scols), BF16),
     ]
     dma = pltpu.SemaphoreType.DMA
     sems = [dma((7,)), dma((4,))]

time: 68.9 us -> 68.5 us (level)
  no operation moved by 1% of the time
where the time goes in v10:
time: 68.5 us; the launch traced here: 68.4 us
  Pallas kernels  67.7 us (99%)
    pallas_call x1, Pallas kernels, body(): pl.pallas_call(functools.partial(kernel, d), out_shape=(jax.ShapeDtypeStr...  65.4 us
    pallas_call x1, Pallas kernels, body(): pl.pallas_call(functools.partial(unpack, d), out_shape=(jax.ShapeDtypeStr...  2.29 us

profile of v10, /device:TPU:1, one launch (start us, length us, event | category | flops | bytes accessed | tf_op | source)
XLA Modules:
  0.0 68.4 jit_solution(15167593955523910424)
XLA Ops:
  0.6 65.4 %shard_map.102 = (f32[256,128]{1,0:T(8,128)}, f32[512,128]{1,0:T(8,128)}, bf16[2,16,16,512]{3,2,1,0:T(8,128)(2,1)}) custom-call(bf16[256,128]{1,0:T(8,128)(2,1)} %users_in.1, bf16[256]{0:T(256)(128)(2,1)} %weight_in.1, s32[256]{0:T(256)} %pos_in.1, bf16[512,128]{1,0:T(8,128)(2,1)} %feats_in.1, s32[512]{0:T(512)} %valid_in.1, bf16[128,1024]{1,0:T(8,128)(2,1)} %w_in_in.1, ...), custom_call_target="tpu_custom_call" | custom-call | flops 3221225472 | bytes 4194304 | tf_op jit(solution)/shard_map/pallas_call | solution.py:690
  66.1 2.3 %shard_map.103 = (f32[256,128]{1,0:T(8,128)}, f32[512,128]{1,0:T(8,128)}, f32[128,1024]{1,0:T(8,128)}, f32[1024,128]{1,0:T(8,128)}) custom-call(f32[256,128]{1,0:T(8,128)} %get-tuple-element.7.user_ref, f32[512,128]{1,0:T(8,128)} %get-tuple-element.8.item_ref, bf16[2,2,8,16,512]{4,3,2,1,0:T(8,128)(2,1)} %bitcast.1), custom_call_target="tpu_custom_call" | custom-call | tf_op jit(solution)/shard_map/pallas_call | solution.py:711
